TPU v7x, 128 devices: a whole 4x4x4 slice. The times are simulated.
128 devices in a mesh: grp: 32 (over x, y, z_lo), mem: 4 (over z_hi, core).
Axes of the slice: x: 4, y: 4, z: 4 (z_hi: 2, z_lo: 2; z = z_hi * 2 + z_lo), core: 2. Of those that a mesh axis runs over, the one named last changes fastest.
Arguments:
- points: float32 [11, 32768], P(None, ('grp', 'mem')), may hold values from -6 to 6
- inv_length: float32 [11], replicated, may hold values from 0.15 to 0.6
- out_scale: float32 [1], replicated, may hold values from 0.5 to 2
- noise: float32 [1], replicated, may hold values from 0.5 to 1.5
- solution: float32 [8, 32768], P(None, ('grp', 'mem')), may hold values from -6 to 6
- residual: float32 [8, 32768], P(None, ('grp', 'mem')), may hold values from -6 to 6
- direction: float32 [8, 32768], P(None, ('grp', 'mem')), may hold values from -6 to 6
Outputs:
- solution_out: float32 [8, 32768], P(None, ('grp', 'mem'))
- residual_out: float32 [8, 32768], P(None, ('grp', 'mem'))
- direction_out: float32 [8, 32768], P(None, ('grp', 'mem'))
All inputs are finite; a program needn't handle non-finite values.
Results may differ from a plain program's by a relative error of at most 0.0003.
Values sent between devices are 32-bit elements; how exact they have to be, the bound alone decides.
A program may use at most 128 MiB of HBM per device.

v0:
```python
import jax
import jax.numpy as jnp
from jax import lax
from jax.sharding import PartitionSpec as P

ITERS = 2


HIGH = lax.Precision.HIGHEST


def kernel_tile(rows_scaled, rows_sq, cols_scaled, out_scale):
    cols_sq = jnp.sum(cols_scaled * cols_scaled, axis=0)
    cross = lax.dot_general(rows_scaled, cols_scaled, (((0,), (0,)), ((), ())), precision=HIGH)
    dist_sq = jnp.maximum(rows_sq[:, None] + cols_sq[None, :] - 2.0 * cross, 0.0)
    radius = jnp.sqrt(5.0 * dist_sq)
    return out_scale[0] * (1.0 + radius + radius * radius / 3.0) * jnp.exp(-radius)


def forward(tile, col_vectors):
    return lax.dot_general(col_vectors, tile, (((1,), (1,)), ((), ())), precision=HIGH)


def per_device(points, inv_length, out_scale, noise, solution, residual, direction):
    scaled = points * inv_length[:, None]
    own_sq = jnp.sum(scaled * scaled, axis=0)
    group_scaled = lax.all_gather(scaled, "mem", axis=1, tiled=True)
    norm_now = lax.psum(jnp.sum(residual * residual, axis=1), ("grp", "mem"))
    for step in range(ITERS):
        group_vectors = lax.all_gather(direction, "mem", axis=1, tiled=True)
        tile = kernel_tile(
            scaled, own_sq, lax.all_gather(group_scaled, "grp", axis=1, tiled=True), out_scale
        )
        image = forward(tile, lax.all_gather(group_vectors, "grp", axis=1, tiled=True))
        image = image + noise[0] * direction
        curve = lax.psum(jnp.sum(direction * image, axis=1), ("grp", "mem"))
        alpha = norm_now / curve
        solution = solution + alpha[:, None] * direction
        residual = residual - alpha[:, None] * image
        norm_next = lax.psum(jnp.sum(residual * residual, axis=1), ("grp", "mem"))
        direction = residual + (norm_next / norm_now)[:, None] * direction
        norm_now = norm_next
    return (solution, residual, direction)


def solution(mesh):
    placed = (
        P(None, ("grp", "mem")),
        P(),
        P(),
        P(),
        P(None, ("grp", "mem")),
        P(None, ("grp", "mem")),
        P(None, ("grp", "mem")),
    )
    return jax.shard_map(
        per_device,
        mesh=mesh,
        in_specs=placed,
        out_specs=(P(None, ("grp", "mem")), P(None, ("grp", "mem")), P(None, ("grp", "mem"))),
        check_vma=False,
    )
```

profile of v0, /device:TPU:1, one launch (start us, length us, event | category | flops | bytes accessed | tf_op | source)
XLA Modules:
  0.0 806.4 jit_solution(16958656086224337856)
XLA Ops:
  7.2 0.0 all-gather.4.cloned.1.call-start
  7.2 0.8 multiply_reduce_fusion.1
  8.0 9.0 %all_gather.19 = f32[11,1024]{1,0:T(8,128)} all-gather(f32[11,256]{1,0:T(8,128)S(1)} %get-tuple-element.10), channel_id=1, replica_groups=mesh['grp'=32,'mem'=4] {'mem'}, dimensions={1}, use_global_device_ids=true | all-gather | bytes 56320 | tf_op jit(solution)/shard_map/all_gather | solution.py:27
  17.0 0.0 all-gather.4.cloned.1.call-update
  17.0 0.0 all-gather.6.cloned.1.call-start
  17.1 8.6 %all_gather.21 = f32[8,1024]{1,0:T(8,128)} all-gather(f32[8,256]{1,0:T(8,128)} %param.13), channel_id=1, replica_groups=mesh['grp'=32,'mem'=4] {'mem'}, dimensions={1}, use_global_device_ids=true | all-gather | bytes 40960 | tf_op jit(solution)/shard_map/all_gather | solution.py:30
  25.7 0.0 all-gather.6.cloned.1.call-update
  25.7 0.0 all-gather.8.cloned.1.call-start
  27.0 0.8 multiply_reduce_fusion.6
  27.8 123.6 %all-gather.4.cloned.1.call-done = f32[11,32768]{1,0:T(8,128)} async-done(((f32[11,1024]{1,0:T(8,128)}), f32[11,32768]{1,0:T(8,128)}) %all-gather.4.cloned.1.call-update) | async-done | bytes 1441808 | tf_op jit(solution)/shard_map/all_gather | solution.py:32
  151.4 2.0 multiply_reduce_fusion
  153.4 0.0 copy-start
  153.4 51.5 %exponential_multiply_fusion = f32[256,32768]{1,0:T(8,128)} fusion(f32[11,256]{1,0:T(8,128)S(1)} %get-tuple-element.10, f32[11,32768]{1,0:T(8,128)} %all-gather.4.cloned.1.call-done, f32[32768]{0:T(1024)S(1)} %multiply_reduce_fusion, f32[256]{0:T(256)S(1)} %get-tuple-element.9, f32[]{:T(128)} %bitcast.12), kind=kOutput, calls=%fused_computation.5 | convolution fusion | flops 1207959552 | bytes 35139588 | tf_op jit(solution)/shard_map/dot_general | solution.py:14
  204.9 0.0 copy-start.2
  204.9 97.4 %all-gather.6.cloned.1.call-done = f32[8,32768]{1,0:T(8,128)} async-done(((f32[8,1024]{1,0:T(8,128)}), f32[8,32768]{1,0:T(8,128)}) %all-gather.6.cloned.1.call-update) | async-done | bytes 1048592 | tf_op jit(solution)/shard_map/all_gather | solution.py:34
  302.3 0.0 copy-done
  302.3 0.0 copy-start.3
  302.3 29.9 %multiply_reduce_fusion.5 = (f32[8]{0:T(128)S(1)}, f32[8,256]{1,0:T(8,128)S(1)}) fusion(f32[8,256]{1,0:T(8,128)S(1)} %copy-done, f32[]{:T(128)} %bitcast.13, f32[256,32768]{1,0:T(8,128)} %exponential_multiply_fusion, f32[8,32768]{1,0:T(8,128)} %all-gather.6.cloned.1.call-done), kind=kOutput, calls=%fused_computation.19 | convolution fusion | flops 805314560 | bytes 34619428 | tf_op jit(solution)/shard_map/dot_general | solution.py:21
  332.2 86.5 %all-reduce = (f32[8]{0:T(128)S(1)}, f32[8]{0:T(128)S(1)}) all-reduce(f32[8]{0:T(128)S(1)} %multiply_reduce_fusion.6, f32[8]{0:T(128)S(1)} %get-tuple-element.13), channel_id=1, replica_groups=mesh['grp'=32,'mem'=4] {'grp','mem'}, use_global_device_ids=true, to_apply=%region_1.0 | all-reduce | flops 16 | bytes 128 | tf_op jit(solution)/shard_map/psum | solution.py:28
  418.6 0.0 copy-done.2
  418.6 0.2 multiply_reduce_fusion.4
  418.8 64.4 %psum.37 = f32[8]{0:T(128)S(1)} all-reduce(f32[8]{0:T(128)S(1)} %get-tuple-element.7), channel_id=1, replica_groups=mesh['grp'=32,'mem'=4] {'grp','mem'}, use_global_device_ids=true, to_apply=%region_7.0 | all-reduce | flops 8 | bytes 64 | tf_op jit(solution)/shard_map/psum | solution.py:40
  483.3 0.1 multiply_add_fusion.2
  483.3 8.0 all_gather.23
  491.3 0.0 all-gather.8.cloned.1.call-update
  491.4 124.6 %all-gather.8.cloned.1.call-done = f32[8,32768]{1,0:T(8,128)} async-done(((f32[8,1024]{1,0:T(8,128)}), f32[8,32768]{1,0:T(8,128)}) %all-gather.8.cloned.1.call-update) | async-done | bytes 1048592 | tf_op jit(solution)/shard_map/all_gather | solution.py:34
  616.0 32.2 %multiply_reduce_fusion.3 = (f32[8]{0:T(128)S(1)}, f32[8,256]{1,0:T(8,128)S(1)}) fusion(f32[8,256]{1,0:T(8,128)S(1)} %multiply_add_fusion.2, f32[]{:T(128)} %bitcast.14, f32[8,32768]{1,0:T(8,128)} %all-gather.8.cloned.1.call-done, f32[256,32768]{1,0:T(8,128)} %exponential_multiply_fusion), kind=kOutput, calls=%fused_computation.15 | convolution fusion | flops 805314560 | bytes 34619428 | tf_op jit(solution)/shard_map/dot_general | solution.py:21
  648.2 86.3 %psum.38 = f32[8]{0:T(128)S(1)} all-reduce(f32[8]{0:T(128)S(1)} %get-tuple-element.15), channel_id=1, replica_groups=mesh['grp'=32,'mem'=4] {'grp','mem'}, use_global_device_ids=true, to_apply=%region_9.0 | all-reduce | flops 8 | bytes 64 | tf_op jit(solution)/shard_map/psum | solution.py:36
  734.5 0.2 multiply_reduce_fusion.2
  734.7 0.0 copy-start.1
  734.7 64.4 %psum.39 = f32[8]{0:T(128)S(1)} all-reduce(f32[8]{0:T(128)S(1)} %get-tuple-element.5), channel_id=1, replica_groups=mesh['grp'=32,'mem'=4] {'grp','mem'}, use_global_device_ids=true, to_apply=%region_11.0 | all-reduce | flops 8 | bytes 64 | tf_op jit(solution)/shard_map/psum | solution.py:40
  799.2 0.0 copy-done.3
  799.2 0.7 multiply_add_fusion
  799.8 0.0 copy-done.1
  (4 shorter events, 0.0 us)
Async XLA Ops:
  7.2 144.3 %all-gather.4.cloned.1.call-start = ((), (), s32[]{:S(2)}) async-start(), calls=%async_computation | async-start | bytes 2162688 | tf_op jit(solution)/shard_map/all_gather | solution.py:32
  17.0 285.3 %all-gather.6.cloned.1.call-start = ((), (), s32[]{:S(2)}) async-start(), calls=%async_computation.1 | async-start | bytes 1081344 | tf_op jit(solution)/shard_map/all_gather | solution.py:34
  25.7 590.3 %all-gather.8.cloned.1.call-start = ((), (), s32[]{:S(2)}) async-start(), calls=%async_computation.2 | async-start | bytes 1081344 | tf_op jit(solution)/shard_map/all_gather | solution.py:34
  153.4 148.9 %copy-start = (f32[8,256]{1,0:T(8,128)S(1)}, f32[8,256]{1,0:T(8,128)}, u32[]{:S(2)}) copy-start(f32[8,256]{1,0:T(8,128)} %param.13) | copy-start | bytes 24580
  204.9 213.8 %copy-start.2 = (f32[8,256]{1,0:T(8,128)S(1)}, f32[8,256]{1,0:T(8,128)}, u32[]{:S(2)}) copy-start(f32[8,256]{1,0:T(8,128)} %param.12) | copy-start | bytes 24580
  302.3 496.9 %copy-start.3 = (f32[8,256]{1,0:T(8,128)S(1)}, f32[8,256]{1,0:T(8,128)}, u32[]{:S(2)}) copy-start(f32[8,256]{1,0:T(8,128)} %param.11) | copy-start | bytes 24580
  734.7 65.1 %copy-start.1 = (f32[8,256]{1,0:T(8,128)}, f32[8,256]{1,0:T(8,128)S(1)}, u32[]{:S(2)}) copy-start(f32[8,256]{1,0:T(8,128)S(1)} %get-tuple-element.6) | copy-start | bytes 24580
Sparse Core Ops, SparseCore 0:
  17.1 134.2 all-gather.3
  153.1 149.1 all-gather.5
  491.5 124.4 all-gather.7
where the time goes:
time: 807 us; the launch traced here: 806 us
  waiting for transfers between devices  346 us (43%)
  blocking collectives  327 us (41%)
  matrix products  114 us (14%)
  between operations  15.1 us (2%)
    all_gather x2, waiting for transfers between devices, per_device(): lax.all_gather(group_vectors, 'grp', axis=1, tiled=True)  222 us
    psum x2, blocking collectives, per_device(): norm_next = lax.psum(jnp.sum(residual * residual, axis=1), ('grp', 'mem'))  129 us
    all_gather x1, waiting for transfers between devices, per_device(): lax.all_gather(group_scaled, 'grp', axis=1, tiled=True)  124 us
    psum x1, blocking collectives, per_device(): norm_now = lax.psum(jnp.sum(residual * residual, axis=1), ('grp', 'mem'))  86.5 us
    psum x1, blocking collectives, per_device(): curve = lax.psum(jnp.sum(direction * image, axis=1), ('grp', 'mem'))  86.3 us
    dot_general x2, matrix products, forward(): lax.dot_general(col_vectors, tile, (((1,), (1,)), ((), ())), precision=HIGH)  62.1 us
    dot_general x1, matrix products, kernel_tile(): lax.dot_general(rows_scaled, cols_scaled, (((0,), (0,)), ((), ())), preci...  51.5 us
    all_gather x2, blocking collectives, per_device(): group_vectors = lax.all_gather(direction, 'mem', axis=1, tiled=True)  16.6 us
  transfers between devices with their start and end apart: 3, of which 3 were waited for; matrix products, arithmetic and copies ran while one was open for 7% of the time, Pallas kernels for 0%

commit v1 on v0

v1 whole, which is shorter than its diff:
```python
import functools
import math
import random

import jax
import jax.numpy as jnp
from jax import lax
from jax.experimental import pallas as pl
from jax.experimental.pallas import tpu as pltpu
from jax.sharding import PartitionSpec as P

MESH = pl.DeviceIdType.MESH
f32 = jnp.float32
bf16 = jnp.bfloat16

FEAT = 11
VEC = 8
COLS = 256
CHIPS = 64
GROUP = 8
LOG2E = math.log2(math.e)
LIFT = 1.5 * LOG2E
SHIFT = 0.75 * LOG2E * LOG2E
SCALE = math.exp(1.5) / (3.0 * LOG2E * LOG2E)


def hops(off):
    return sum((0, 1, 2, 1)[d] for d in off)


def offsets():
    every = [(i, j, k) for i in range(4) for j in range(4) for k in range(4)]
    random.Random(1).shuffle(every)
    return sorted(every, key=hops)


OFFS = offsets()


def split3(rows):
    high = rows.astype(bf16)
    rest = rows - high.astype(f32)
    mid = rest.astype(bf16)
    low = (rest - mid.astype(f32)).astype(bf16)
    return high, mid, low


def col_stack(rows):
    h, m, l = split3(rows)
    return jnp.concatenate([h, h, m, m, h, l, jnp.zeros((32, rows.shape[1]), bf16)], 0)


def row_stack(rows):
    h, m, l = split3(rows)
    return jnp.concatenate([h, m, h, m, l, h, jnp.zeros((32, rows.shape[1]), bf16)], 0)


def vec_stack(rows):
    high = rows.astype(bf16).astype(f32)
    return jnp.concatenate([high, rows - high], 0).astype(bf16)


def tile_of(t):
    t = jnp.maximum(t, 1e-30)
    w = -LIFT - t * lax.rsqrt(t)
    return (w * w + SHIFT) * jnp.exp2(w)


def mv(x, k):
    return jnp.dot(x, k, preferred_element_type=f32)


def fold(acc):
    return acc[0:VEC] + acc[VEC : 2 * VEC]


def kernel(
    pts, inv, oscale, noise, sol, res, dirn,
    sol_out, res_out, dir_out,
    snd, rsnd, isnd, fsnd, gath, rgath, igath, fgath,
    qmat, khi, klo, acc_d, acc_r, acc_i, dots,
    ex_s, ex_p, ex_a, ex_b, ex_c, ex_d, ex_e,
    s_p, r_p, s_r, r_r, s_i, r_i, s_f, r_f, s_x, r_x,
):
    g, m = lax.axis_index("grp"), lax.axis_index("mem")
    x, y, z, core = g // 8, (g // 2) % 4, (m // 2) * 2 + g % 2, m % 2
    xs = [((x + d) % 4) * 8 for d in range(4)]
    ys = [((y + d) % 4) * 2 for d in range(4)]
    zs = [(z + d) % 4 for d in range(4)]
    zg = [v % 2 for v in zs]
    zm = [(v // 2) * 2 + core for v in zs]
    partner = (g, (m // 2) * 2 + 1 - core)

    def peer(k):
        dx, dy, dz = OFFS[k]
        return (xs[dx] + ys[dy] + zg[dz], zm[dz])

    barrier = pltpu.get_barrier_semaphore()
    pl.semaphore_signal(barrier, inc=1, device_id=partner, device_id_type=MESH)
    for k in range(1, CHIPS):
        pl.semaphore_signal(barrier, inc=1, device_id=peer(k), device_id_type=MESH)

    gain = math.sqrt(5.0) * LOG2E
    snd[...] = jnp.zeros_like(snd)
    for f in range(FEAT):
        snd[f : f + 1, :] = pts[f : f + 1, :] * (inv[f] * gain)
    scaled = snd[0:16, :]
    snd[11:12, :] = jnp.sum(scaled * scaled, axis=0, keepdims=True)
    snd[12:13, :] = jnp.ones((1, COLS), f32)
    snd[16:24, :] = dirn[...]
    rsnd[...] = res[...]

    def exchange(n, src, dst):
        cp = pltpu.make_async_remote_copy(
            src_ref=src, dst_ref=dst, send_sem=s_x.at[n], recv_sem=r_x.at[n],
            device_id=partner, device_id_type=MESH,
        )
        cp.start()
        return cp

    def spread(src, dst, s, r, start=True):
        own = pltpu.make_async_copy(src, dst.at[0], r.at[0])
        cps = [own]
        for k in range(1, CHIPS):
            cps.append(
                pltpu.make_async_remote_copy(
                    src_ref=src, dst_ref=dst.at[k], send_sem=s.at[k], recv_sem=r.at[k],
                    device_id=peer(k), device_id_type=MESH,
                )
            )
        for cp in cps:
            cp.start()

    def arrived(grp, src, dst, s, r):
        for u in range(GROUP):
            k = grp * GROUP + u
            pltpu.make_async_copy(src, dst.at[k], r.at[k]).wait()

    def sent(src, dst, s, r):
        for k in range(1, CHIPS):
            pltpu.make_async_copy(src, dst.at[k], s.at[k]).wait()

    pl.semaphore_wait(barrier, CHIPS)
    cp_p = exchange(0, snd.at[pl.ds(0, 16)], ex_p)
    spread(snd, gath, s_p, r_p)
    spread(rsnd, rgath, s_r, r_r)

    row = lax.broadcasted_iota(jnp.int32, (16, COLS), 0)

    def rows_side(blk):
        swapped = jnp.where(row == 11, 1.0, jnp.where(row == 12, blk[11:12, :], 0.0))
        return row_stack(jnp.where(row < FEAT, -2.0 * blk, swapped))

    qmat[:, 0:COLS] = rows_side(snd[0:16, :])
    cp_p.wait()
    qmat[:, COLS : 2 * COLS] = rows_side(ex_p[...])

    acc_d[...] = jnp.zeros_like(acc_d)
    acc_r[...] = jnp.zeros_like(acc_r)
    acc_i[...] = jnp.zeros_like(acc_i)
    dots[...] = jnp.zeros_like(dots)

    @pl.loop(0, CHIPS // GROUP)
    def _(grp):
        arrived(grp, snd, gath, s_p, r_p)
        for u in range(GROUP):
            k = grp * GROUP + u
            cols = col_stack(gath[k, 0:16, :])
            vec = vec_stack(gath[k, 16:24, :])
            for i0 in range(0, 2 * COLS, 256):
                part = acc_d[:, i0 : i0 + 256]
                for j0 in range(0, COLS, 128):
                    t = lax.dot_general(
                        cols[:, j0 : j0 + 128], qmat[:, i0 : i0 + 256],
                        (((0,), (0,)), ((), ())), preferred_element_type=f32,
                    )
                    tile = tile_of(t)
                    hi = tile.astype(bf16)
                    lo = (tile - hi.astype(f32)).astype(bf16)
                    khi[k, j0 : j0 + 128, i0 : i0 + 256] = hi
                    klo[k, j0 : j0 + 128, i0 : i0 + 256] = lo
                    v = vec[:, j0 : j0 + 128]
                    part = part + mv(v, hi) + mv(v, lo)
                acc_d[:, i0 : i0 + 256] = part

    def times(acc, src, grp):
        for i0 in range(0, 2 * COLS, 256):
            part = acc[:, i0 : i0 + 256]
            for u in range(GROUP):
                k = grp * GROUP + u
                v = vec_stack(src[k])
                part = part + mv(v, khi[k, :, i0 : i0 + 256]) + mv(v, klo[k, :, i0 : i0 + 256])
            acc[:, i0 : i0 + 256] = part

    total = fold(acc_d[...])
    ex_s[...] = total[:, COLS:]
    cp_a = exchange(1, ex_s, ex_a)
    cp_a.wait()
    kd = (SCALE * oscale[0]) * (total[:, :COLS] + ex_a[...])
    image = kd + noise[0] * dirn[...]
    isnd[...] = image
    spread(isnd, igath, s_i, r_i)

    @pl.loop(0, CHIPS // GROUP)
    def _(grp):
        arrived(grp, rsnd, rgath, s_r, r_r)
        times(acc_r, rgath, grp)

    sent(snd, gath, s_p, r_p)
    sent(rsnd, rgath, s_r, r_r)

    @pl.loop(0, CHIPS // GROUP)
    def _(grp):
        arrived(grp, isnd, igath, s_i, r_i)
        rr, di = dots[0], dots[1]
        for u in range(GROUP):
            k = grp * GROUP + u
            r, d, im = rgath[k], gath[k, 16:24, :], igath[k]
            rr = rr + r * r
            di = di + d * im
        dots[0] = rr
        dots[1] = di
        times(acc_i, igath, grp)

    lane = lax.broadcasted_iota(jnp.int32, (VEC, 128), 1)

    def pack(*cols):
        out = jnp.zeros((VEC, 128), f32)
        for n, c in enumerate(cols):
            out = jnp.where(lane == n, c, out)
        return out

    def take(a, n):
        return jnp.sum(jnp.where(lane == n, a, 0.0), axis=1, keepdims=True)

    def total_of(a):
        return jnp.sum(a, axis=1, keepdims=True)

    mine = pack(total_of(dots[0]), total_of(dots[1]))
    fsnd[0] = mine
    cp_b = exchange(2, fsnd.at[0], ex_b)
    cp_b.wait()
    both = mine + ex_b[...]
    norm0 = take(both, 0)
    alpha0 = norm0 / take(both, 1)

    def sq_step(k, acc):
        r1 = rgath[k] - alpha0 * igath[k]
        return acc + r1 * r1

    mine = pack(total_of(lax.fori_loop(0, CHIPS, sq_step, jnp.zeros((VEC, COLS), f32))))
    fsnd[1] = mine
    cp_c = exchange(3, fsnd.at[1], ex_c)
    part = fold(acc_r[...]) - alpha0 * fold(acc_i[...])
    ex_s2 = ex_d.at[0]
    ex_s2[...] = part[:, COLS:]
    cp_d = exchange(4, ex_s2, ex_d.at[1])
    cp_c.wait()
    norm1 = take(mine + ex_c[...], 0)
    beta = norm1 / norm0
    r1 = res[...] - alpha0 * image
    d1 = r1 + beta * dirn[...]
    cp_d.wait()
    im1 = (SCALE * oscale[0]) * (part[:, :COLS] + ex_d[1]) + beta * kd + noise[0] * d1
    mine = pack(total_of(d1 * im1), total_of(r1 * im1), total_of(im1 * im1))
    fsnd[2] = mine
    spread(fsnd.at[2], fgath, s_f, r_f)

    sent(isnd, igath, s_i, r_i)
    sol1 = sol[...] + alpha0 * dirn[...]

    for grp in range(CHIPS // GROUP):
        arrived(grp, fsnd.at[2], fgath, s_f, r_f)
    mine = jnp.sum(fgath[...], axis=0)
    fsnd[3] = mine
    cp_e = exchange(5, fsnd.at[3], ex_e)
    cp_e.wait()
    both = mine + ex_e[...]
    alpha1 = norm1 / take(both, 0)
    norm2 = norm1 + alpha1 * (alpha1 * take(both, 2) - 2.0 * take(both, 1))
    r2 = r1 - alpha1 * im1
    sol_out[...] = sol1 + alpha1 * d1
    res_out[...] = r2
    dir_out[...] = r2 + (norm2 / norm1) * d1
    sent(fsnd.at[2], fgath, s_f, r_f)


def per_device(points, inv_length, out_scale, noise, solution, residual, direction):
    vm = pl.BlockSpec(memory_space=pltpu.VMEM)
    sm = pl.BlockSpec(memory_space=pltpu.SMEM)
    out = jax.ShapeDtypeStruct((VEC, COLS), f32)
    V, D = pltpu.VMEM, pltpu.SemaphoreType.DMA
    return pl.pallas_call(
        kernel,
        out_shape=(out, out, out),
        in_specs=[vm, sm, sm, sm, vm, vm, vm],
        out_specs=(vm, vm, vm),
        scratch_shapes=[
            V((24, COLS), f32), V((VEC, COLS), f32), V((VEC, COLS), f32), V((4, VEC, 128), f32),
            V((CHIPS, 24, COLS), f32), V((CHIPS, VEC, COLS), f32),
            V((CHIPS, VEC, COLS), f32), V((CHIPS, VEC, 128), f32),
            V((128, 2 * COLS), bf16),
            V((CHIPS, COLS, 2 * COLS), bf16), V((CHIPS, COLS, 2 * COLS), bf16),
            V((16, 2 * COLS), f32), V((16, 2 * COLS), f32), V((16, 2 * COLS), f32),
            V((2, VEC, COLS), f32),
            V((VEC, COLS), f32), V((16, COLS), f32), V((VEC, COLS), f32),
            V((VEC, 128), f32), V((VEC, 128), f32), V((2, VEC, COLS), f32), V((VEC, 128), f32),
            D((CHIPS,)), D((CHIPS,)), D((CHIPS,)), D((CHIPS,)),
            D((CHIPS,)), D((CHIPS,)), D((CHIPS,)), D((CHIPS,)),
            D((6,)), D((6,)),
        ],
        compiler_params=pltpu.CompilerParams(
            collective_id=0, has_side_effects=True, vmem_limit_bytes=56 * 2**20
        ),
        name="cg",
    )(points, inv_length, out_scale, noise, solution, residual, direction)


def solution(mesh):
    cols = P(None, ("grp", "mem"))
    return jax.shard_map(
        per_device,
        mesh=mesh,
        in_specs=(cols, P(), P(), P(), cols, cols, cols),
        out_specs=(cols, cols, cols),
        check_vma=False,
    )
```

time: 807 us -> 73.8 us (0.09)
  waiting for transfers between devices: 346 us -> 0 us
  blocking collectives: 327 us -> 0 us
  matrix products: 114 us -> 0 us
  Pallas kernels: 0 us -> 69 us
  between operations: 15.1 us -> 1.94 us
    all_gather x3 -> x0, waiting for transfers between devices: 346 us -> none  [the longest x2 222 us: per_device(): lax.all_gather(group_vectors, 'grp', axis=1, tiled=True)]
    psum x4 -> x0, blocking collectives: 302 us -> none  [the longest x2 129 us: per_device(): norm_next = lax.psum(jnp.sum(residual * residual, axis=1), ('grp', 'mem'))]
    dot_general x3 -> x0, matrix products: 114 us -> none  [the longest x2 62.1 us: forward(): lax.dot_general(col_vectors, tile, (((1,), (1,)), ((), ())), precision=HIGH)]
    pallas_call x0 -> x1, Pallas kernels: none -> 69 us  [per_device(): pl.pallas_call(kernel, out_shape=(out, out, out), in_specs=[vm, sm, sm, s...]
    all_gather x3 -> x0, blocking collectives: 25.6 us -> none  [the longest x2 16.6 us: per_device(): group_vectors = lax.all_gather(direction, 'mem', axis=1, tiled=True)]
  transfers between devices with their start and end apart: 3 -> 0, of which waited for: 3 -> 0; matrix products, arithmetic and copies ran while one was open for 7% -> 0% of each run, Pallas kernels for 0% -> 0%
where the time goes in v1:
time: 73.8 us; the launch traced here: 73.6 us
  Pallas kernels  69 us (93%)
  local copies, waits for them, and re-layouts  2.6 us (4%)
  between operations  1.94 us (3%)
    pallas_call x1, Pallas kernels, per_device(): pl.pallas_call(kernel, out_shape=(out, out, out), in_specs=[vm, sm, sm, s...  69 us
    unnamed x7, local copies, waits for them, and re-layouts  2.6 us

profile of v1, /device:TPU:1, one launch (start us, length us, event | category | flops | bytes accessed | tf_op | source)
XLA Modules:
  0.0 73.6 jit_solution(2626774361467411350)
XLA Ops:
  1.9 69.0 %cg.1 = (f32[8,256]{1,0:T(8,128)}, f32[8,256]{1,0:T(8,128)}, f32[8,256]{1,0:T(8,128)}) custom-call(f32[11,256]{1,0:T(8,128)} %pts.1, f32[11]{0:T(128)} %inv.1, f32[1]{0:T(128)S(6)} %copy.13.oscale, f32[1]{0:T(128)S(6)} %copy.14.noise, f32[8,256]{1,0:T(8,128)} %sol.1, f32[8,256]{1,0:T(8,128)} %res.1, f32[8,256]{1,0:T(8,128)} %dirn.1), custom_call_target="tpu_custom_call" | custom-call | tf_op jit(solution)/shard_map/cg/pallas_call | solution.py:293
  71.0 0.0 copy-start.1
  71.0 1.3 %copy.15 = f32[8,256]{1,0:T(8,128)} copy(f32[8,256]{1,0:T(8,128)} %get-tuple-element.6) | data formatting | bytes 16384
  72.3 0.0 copy-done.1
  72.3 0.0 copy-start
  72.3 0.6 copy.16
  72.9 0.1 copy-done
  73.0 0.6 copy.17
Async XLA Ops:
  71.0 1.3 %copy-start.1 = (f32[8,256]{1,0:T(8,128)S(1)}, f32[8,256]{1,0:T(8,128)}, u32[]{:S(2)}) copy-start(f32[8,256]{1,0:T(8,128)} %get-tuple-element.7) | copy-start | bytes 24580
  72.3 0.7 copy-start

commit v2 on v1

v2 whole, which is shorter than its diff:
```python
import math
import random

import jax
import jax.numpy as jnp
from jax import lax
from jax.experimental import pallas as pl
from jax.experimental.pallas import tpu as pltpu
from jax.sharding import PartitionSpec as P

MESH = pl.DeviceIdType.MESH
f32 = jnp.float32
bf16 = jnp.bfloat16

FEAT = 11
VEC = 8
COLS = 256
CHIPS = 64
GROUPS = 7
LOG2E = math.log2(math.e)
LIFT = 1.5 * LOG2E
SHIFT = 0.75 * LOG2E * LOG2E
SCALE = math.exp(1.5) / (3.0 * LOG2E * LOG2E)


def offsets():
    every = [(i, j, k) for k in range(4) for j in range(4) for i in range(4)]
    random.Random(1).shuffle(every)
    return sorted(every, key=lambda o: -sum((0, 1, 2, 1)[d] for d in o))[:-1]


OFFS = offsets()


def split3(rows):
    high = rows.astype(bf16)
    rest = rows - high.astype(f32)
    mid = rest.astype(bf16)
    low = (rest - mid.astype(f32)).astype(bf16)
    return high, mid, low


def col_stack(rows):
    h, m, l = split3(rows)
    return jnp.concatenate([h, h, m, m, h, l, jnp.zeros((32, rows.shape[1]), bf16)], 0)


def row_stack(rows):
    h, m, l = split3(rows)
    return jnp.concatenate([h, m, h, m, l, h, jnp.zeros((32, rows.shape[1]), bf16)], 0)


def vec_stack(rows):
    high = rows.astype(bf16).astype(f32)
    return jnp.concatenate([high, rows - high], 0).astype(bf16)


def tile_of(t):
    t = jnp.maximum(t, 1e-30)
    w = -LIFT - t * lax.rsqrt(t)
    return (w * w + SHIFT) * jnp.exp2(w)


def mv(x, k):
    return jnp.dot(x, k, preferred_element_type=f32)


def fold(acc):
    return acc[0:VEC] + acc[VEC : 2 * VEC]


def kernel(
    pts, inv, oscale, noise, sol, res, dirn,
    sol_out, res_out, dir_out,
    gath, igath, fgath, isnd, fsnd,
    qmat, khi, klo, acc_d, acc_r, acc_i, dots,
    ex_p, ex_s, ex_r, sc_s, sc_r,
    s_line, r_line, s_run, r_run, s_one, r_one,
    s_i, r_i, s_f, r_f, s_x, r_x,
):
    g, m = lax.axis_index("grp"), lax.axis_index("mem")
    x, y, z, core = g // 8, (g // 2) % 4, (m // 2) * 2 + g % 2, m % 2
    partner = (g, (m // 2) * 2 + 1 - core)

    def peer(e1, e2, e3):
        px = (x + e1 + core * (e3 - e1)) % 4
        py = (y + e2) % 4
        pz = (z + e3 + core * (e1 - e3)) % 4
        return ((px * 4 + py) * 2 + pz % 2, (pz // 2) * 2 + core)

    barrier = pltpu.get_barrier_semaphore()

    def greet(device):
        pl.semaphore_signal(barrier, inc=1, device_id=device, device_id_type=MESH)

    greet(partner)
    for e in (1, 3, 2):
        greet(peer(e, 0, 0))
        greet(peer(0, e, 0))
        greet(peer(0, 0, e))

    gain = math.sqrt(5.0) * LOG2E
    own = gath.at[0, 0, 0]
    own[0:16, :] = jnp.zeros((16, COLS), f32)
    for f in range(FEAT):
        own[f : f + 1, :] = pts[f : f + 1, :] * (inv[f] * gain)
    scaled = own[0:16, :]
    own[11:12, :] = jnp.sum(scaled * scaled, axis=0, keepdims=True)
    own[12:13, :] = jnp.ones((1, COLS), f32)
    own[16:24, :] = dirn[...]
    own[24:32, :] = res[...]

    def put(src, dst, s, r, device):
        cp = pltpu.make_async_remote_copy(
            src_ref=src, dst_ref=dst, send_sem=s, recv_sem=r, device_id=device, device_id_type=MESH
        )
        cp.start()
        return cp

    def await_(ref, sem):
        pltpu.make_async_copy(ref, ref, sem).wait()

    def exchange(n, src, dst):
        return put(src, dst, s_x.at[n], r_x.at[n], partner)

    def run(e3, e2):
        return gath.at[e3, e2, pl.ds(1, 3)]

    def one(e3, e2):
        return gath.at[e3, e2, 0]

    pl.semaphore_wait(barrier, 10)
    cp_p = exchange(0, own.at[pl.ds(0, 16)], ex_p)
    for e in (1, 3, 2):
        put(own, gath.at[0, 0, e], s_line.at[e], r_line.at[e], peer(e, 0, 0))
        put(own, one(0, e), s_one.at[e], r_one.at[e], peer(0, e, 0))
        put(own, one(e, 0), s_one.at[4 * e], r_one.at[4 * e], peer(0, 0, e))

    row = lax.broadcasted_iota(jnp.int32, (16, COLS), 0)

    def rows_side(blk):
        swapped = jnp.where(row == 11, 1.0, jnp.where(row == 12, blk[11:12, :], 0.0))
        return row_stack(jnp.where(row < FEAT, -2.0 * blk, swapped))

    acc_d[...] = jnp.zeros_like(acc_d)
    acc_r[...] = jnp.zeros_like(acc_r)
    acc_i[...] = jnp.zeros_like(acc_i)
    dots[...] = jnp.zeros_like(dots)
    qmat[:, 0:COLS] = rows_side(own[0:16, :])
    cp_p.wait()
    qmat[:, COLS : 2 * COLS] = rows_side(ex_p[...])

    def build(places):
        for e3, e2, e1 in places:
            k = e3 * 16 + e2 * 4 + e1
            cols = col_stack(gath[e3, e2, e1, 0:16, :])
            vec = vec_stack(gath[e3, e2, e1, 16:24, :])
            for i0 in range(0, 2 * COLS, 256):
                part = acc_d[:, i0 : i0 + 256]
                for j0 in range(0, COLS, 128):
                    t = lax.dot_general(
                        cols[:, j0 : j0 + 128], qmat[:, i0 : i0 + 256],
                        (((0,), (0,)), ((), ())), preferred_element_type=f32,
                    )
                    tile = tile_of(t)
                    hi = tile.astype(bf16)
                    lo = (tile - hi.astype(f32)).astype(bf16)
                    khi[k, j0 : j0 + 128, i0 : i0 + 256] = hi
                    klo[k, j0 : j0 + 128, i0 : i0 + 256] = lo
                    v = vec[:, j0 : j0 + 128]
                    part = part + mv(v, hi) + mv(v, lo)
                acc_d[:, i0 : i0 + 256] = part

    def times(acc, places, rows_of):
        for i0 in range(0, 2 * COLS, 256):
            part = acc[:, i0 : i0 + 256]
            for e3, e2, e1 in places:
                k = e3 * 16 + e2 * 4 + e1
                v = vec_stack(rows_of(e3, e2, e1))
                part = part + mv(v, khi[k, :, i0 : i0 + 256]) + mv(v, klo[k, :, i0 : i0 + 256])
            acc[:, i0 : i0 + 256] = part

    def pick(grp, *cases):
        out = cases[-1]
        for n in range(len(cases) - 2, -1, -1):
            out = jnp.where(grp == n, cases[n], out)
        return out

    def third(grp):
        return pick(grp, 0, 0, 0, 0, 1, 3, 2)

    def places_of(grp):
        e = third(grp)
        return [
            (
                pick(grp, p if q == 3 else 0, 0, q, q, e),
                pick(grp, p if q == 2 else 0, q, 0, p, q),
                pick(grp, p if q == 1 else 0, p, p, 0, p),
            )
            for q in range(1, 4)
            for p in range(1, 4)
        ]

    build([(0, 0, 0)])

    for e in (1, 3, 2):
        await_(own, r_line.at[e])
    for e in (1, 3, 2):
        put(run(0, 0), run(0, e), s_run.at[e], r_run.at[e], peer(0, e, 0))
        put(run(0, 0), run(e, 0), s_run.at[4 * e], r_run.at[4 * e], peer(0, 0, e))
    for e in (1, 3, 2):
        await_(own, r_one.at[e])
        for f in (1, 3, 2):
            put(one(0, e), one(f, e), s_one.at[4 * f + e], r_one.at[4 * f + e], peer(0, 0, f))
    for e in (1, 3, 2):
        await_(own, r_one.at[4 * e])

    @pl.loop(0, GROUPS)
    def _(grp):
        @pl.when(grp == 1)
        def _():
            for e in (1, 3, 2):
                await_(run(0, e), r_run.at[e])
                for f in (1, 3, 2):
                    put(run(0, e), run(f, e), s_run.at[4 * f + e], r_run.at[4 * f + e], peer(0, 0, f))

        @pl.when(grp == 2)
        def _():
            for e in (1, 3, 2):
                await_(run(e, 0), r_run.at[4 * e])

        @pl.when(grp == 3)
        def _():
            for e in (1, 3, 2):
                for f in (1, 3, 2):
                    await_(own, r_one.at[4 * e + f])

        @pl.when(grp >= 4)
        def _():
            e = third(grp)
            for f in (1, 3, 2):
                await_(run(e, f), r_run.at[4 * e + f])

        build(places_of(grp))

    total = fold(acc_d[...])
    ex_s[0] = total[:, COLS:]
    cp_a = exchange(1, ex_s.at[0], ex_r.at[0])
    times(acc_r, [(0, 0, 0)], lambda e3, e2, e1: gath[e3, e2, e1, 24:32, :])
    cp_a.wait()
    kd = (SCALE * oscale[0]) * (total[:, :COLS] + ex_r[0])
    image = kd + noise[0] * dirn[...]
    isnd[...] = image
    igath[0, 0, 0] = image
    for n, (e1, e2, e3) in enumerate(OFFS):
        put(isnd, igath.at[e3, e2, e1], s_i.at[0], r_i.at[e3 * 16 + e2 * 4 + e1], peer(e1, e2, e3))

    @pl.loop(0, GROUPS)
    def _(grp):
        times(acc_r, places_of(grp), lambda e3, e2, e1: gath[e3, e2, e1, 24:32, :])

    def squares(step):
        def one_step(k, acc):
            v = step(k // 16, (k // 4) % 4, k % 4)
            return acc + v

        return lax.fori_loop(0, CHIPS, one_step, jnp.zeros((VEC, COLS), f32), unroll=8)

    def r_of(e3, e2, e1):
        return gath[e3, e2, e1, 24:32, :]

    dots[0] = squares(lambda *e: r_of(*e) * r_of(*e))
    times(acc_i, [(0, 0, 0)], lambda e3, e2, e1: igath[e3, e2, e1])
    dots[1] = dirn[...] * image

    @pl.loop(0, GROUPS)
    def _(grp):
        places = places_of(grp)
        di = dots[1]
        for e3, e2, e1 in places:
            await_(isnd, r_i.at[e3 * 16 + e2 * 4 + e1])
        for e3, e2, e1 in places:
            di = di + gath[e3, e2, e1, 16:24, :] * igath[e3, e2, e1]
        dots[1] = di
        times(acc_i, places, lambda e3, e2, e1: igath[e3, e2, e1])

    lane = lax.broadcasted_iota(jnp.int32, (VEC, 128), 1)
    sub = lax.broadcasted_iota(jnp.int32, (VEC, 128), 0)

    def pack(*cols):
        out = jnp.zeros((VEC, 128), f32)
        for n, c in enumerate(cols):
            out = jnp.where(lane == n * VEC + sub, c, out)
        return jnp.sum(out, axis=0, keepdims=True)

    def take(a, n):
        return jnp.sum(jnp.where(lane == n * VEC + sub, a, 0.0), axis=1, keepdims=True)

    def total_of(a):
        return jnp.sum(a, axis=1, keepdims=True)

    mine = pack(total_of(dots[0]), total_of(dots[1]))
    sc_s[0] = mine
    cp_b = exchange(2, sc_s.at[0], sc_r.at[0])
    cp_b.wait()
    both = mine + sc_r[0]
    norm0 = take(both, 0)
    alpha0 = norm0 / take(both, 1)

    def r1_sq(e3, e2, e1):
        r1 = r_of(e3, e2, e1) - alpha0 * igath[e3, e2, e1]
        return r1 * r1

    mine = pack(total_of(squares(r1_sq)))
    sc_s[1] = mine
    cp_c = exchange(3, sc_s.at[1], sc_r.at[1])
    part = fold(acc_r[...]) - alpha0 * fold(acc_i[...])
    ex_s[1] = part[:, COLS:]
    cp_d = exchange(4, ex_s.at[1], ex_r.at[1])
    cp_c.wait()
    norm1 = take(mine + sc_r[1], 0)
    beta = norm1 / norm0
    r1 = res[...] - alpha0 * image
    d1 = r1 + beta * dirn[...]
    cp_d.wait()
    im1 = (SCALE * oscale[0]) * (part[:, :COLS] + ex_r[1]) + beta * kd + noise[0] * d1
    mine = pack(total_of(d1 * im1), total_of(r1 * im1), total_of(im1 * im1))
    fsnd[...] = mine
    fgath[0] = mine
    for n, (e1, e2, e3) in enumerate(OFFS):
        k = e3 * 16 + e2 * 4 + e1
        put(fsnd, fgath.at[k], s_f.at[0], r_f.at[k], peer(e1, e2, e3))

    sol1 = sol[...] + alpha0 * dirn[...]
    for e in range(1, 4):
        await_(own, s_line.at[e])
    for e in range(1, 16):
        await_(own, s_one.at[e])
        await_(run(0, 0), s_run.at[e])
    flat = igath.at[pl.ds(1, 3)], igath.at[0, pl.ds(1, 3)], igath.at[0, 0, pl.ds(1, 3)]
    for ref in flat:
        await_(ref, s_i.at[0])

    for k in range(1, CHIPS):
        await_(fsnd, r_f.at[k])
    mine = jnp.sum(fgath[...], axis=0)
    sc_s[2] = mine
    cp_e = exchange(5, sc_s.at[2], sc_r.at[2])
    cp_e.wait()
    both = mine + sc_r[2]
    alpha1 = norm1 / take(both, 0)
    norm2 = norm1 + alpha1 * (alpha1 * take(both, 2) - 2.0 * take(both, 1))
    r2 = r1 - alpha1 * im1
    sol_out[...] = sol1 + alpha1 * d1
    res_out[...] = r2
    dir_out[...] = r2 + (norm2 / norm1) * d1
    await_(fgath.at[pl.ds(1, CHIPS - 1)], s_f.at[0])


def per_device(points, inv_length, out_scale, noise, solution, residual, direction):
    vm = pl.BlockSpec(memory_space=pltpu.VMEM)
    sm = pl.BlockSpec(memory_space=pltpu.SMEM)
    out = jax.ShapeDtypeStruct((VEC, COLS), f32)
    V, D = pltpu.VMEM, pltpu.SemaphoreType.DMA
    return pl.pallas_call(
        kernel,
        out_shape=(out, out, out),
        in_specs=[vm, sm, sm, sm, vm, vm, vm],
        out_specs=(vm, vm, vm),
        scratch_shapes=[
            V((4, 4, 4, 32, COLS), f32), V((4, 4, 4, VEC, COLS), f32), V((CHIPS, 1, 128), f32),
            V((VEC, COLS), f32), V((1, 128), f32),
            V((128, 2 * COLS), bf16),
            V((CHIPS, COLS, 2 * COLS), bf16), V((CHIPS, COLS, 2 * COLS), bf16),
            V((16, 2 * COLS), f32), V((16, 2 * COLS), f32), V((16, 2 * COLS), f32),
            V((2, VEC, COLS), f32),
            V((16, COLS), f32), V((2, VEC, COLS), f32), V((2, VEC, COLS), f32),
            V((3, 1, 128), f32), V((3, 1, 128), f32),
            D((4,)), D((4,)), D((16,)), D((16,)), D((16,)), D((16,)),
            D((1,)), D((CHIPS,)), D((1,)), D((CHIPS,)), D((6,)), D((6,)),
        ],
        compiler_params=pltpu.CompilerParams(
            collective_id=0, has_side_effects=True, vmem_limit_bytes=56 * 2**20
        ),
        name="cg",
    )(points, inv_length, out_scale, noise, solution, residual, direction)


def solution(mesh):
    cols = P(None, ("grp", "mem"))
    return jax.shard_map(
        per_device,
        mesh=mesh,
        in_specs=(cols, P(), P(), P(), cols, cols, cols),
        out_specs=(cols, cols, cols),
        check_vma=False,
    )
```

time: 73.8 us -> 65.4 us (0.89)
  Pallas kernels: 69 us -> 60.6 us
    pallas_call x1, Pallas kernels: 69 us -> 60.6 us  [per_device(): pl.pallas_call(kernel, out_shape=(out, out, out), in_specs=[vm, sm, sm, s...]
where the time goes in v2:
time: 65.4 us; the launch traced here: 65.2 us
  Pallas kernels  60.6 us (93%)
  local copies, waits for them, and re-layouts  2.6 us (4%)
  between operations  1.94 us (3%)
    pallas_call x1, Pallas kernels, per_device(): pl.pallas_call(kernel, out_shape=(out, out, out), in_specs=[vm, sm, sm, s...  60.6 us
    unnamed x7, local copies, waits for them, and re-layouts  2.6 us

profile of v2, /device:TPU:1, one launch (start us, length us, event | category | flops | bytes accessed | tf_op | source)
XLA Modules:
  0.0 65.2 jit_solution(7469243701037028526)
XLA Ops:
  1.9 60.6 %cg.1 = (f32[8,256]{1,0:T(8,128)}, f32[8,256]{1,0:T(8,128)}, f32[8,256]{1,0:T(8,128)}) custom-call(f32[11,256]{1,0:T(8,128)} %pts.1, f32[11]{0:T(128)} %inv.1, f32[1]{0:T(128)S(6)} %copy.13.oscale, f32[1]{0:T(128)S(6)} %copy.14.noise, f32[8,256]{1,0:T(8,128)} %sol.1, f32[8,256]{1,0:T(8,128)} %res.1, f32[8,256]{1,0:T(8,128)} %dirn.1), custom_call_target="tpu_custom_call" | custom-call | tf_op jit(solution)/shard_map/cg/pallas_call | solution.py:365
  62.6 0.0 copy-start.1
  62.6 1.3 %copy.15 = f32[8,256]{1,0:T(8,128)} copy(f32[8,256]{1,0:T(8,128)} %get-tuple-element.6) | data formatting | bytes 16384
  63.9 0.0 copy-done.1
  63.9 0.0 copy-start
  63.9 0.6 copy.16
  64.5 0.1 copy-done
  64.6 0.6 copy.17
Async XLA Ops:
  62.6 1.3 %copy-start.1 = (f32[8,256]{1,0:T(8,128)S(1)}, f32[8,256]{1,0:T(8,128)}, u32[]{:S(2)}) copy-start(f32[8,256]{1,0:T(8,128)} %get-tuple-element.7) | copy-start | bytes 24580
  63.9 0.7 %copy-start = (f32[8,256]{1,0:T(8,128)S(1)}, f32[8,256]{1,0:T(8,128)}, u32[]{:S(2)}) copy-start(f32[8,256]{1,0:T(8,128)} %get-tuple-element.8) | copy-start | bytes 24580

commit v3 on v2

v3 whole, which is shorter than its diff:
```python
import math

import jax
import jax.numpy as jnp
from jax import lax
from jax.experimental import pallas as pl
from jax.experimental.pallas import tpu as pltpu
from jax.sharding import PartitionSpec as P

MESH = pl.DeviceIdType.MESH
f32 = jnp.float32
bf16 = jnp.bfloat16

FEAT = 11
VEC = 8
COLS = 256
HALF = 128
CHIPS = 64
GROUPS = 7
LOG2E = math.log2(math.e)
LIFT = 1.5 * LOG2E
SHIFT = 0.75 * LOG2E * LOG2E
SCALE = math.exp(1.5) / (3.0 * LOG2E * LOG2E)


def offsets():
    three = (2, 3, 1)
    out = [(i, j, k) for k in three for j in three for i in three]
    out += [(0, j, k) for k in three for j in three]
    out += [(i, 0, k) for k in three for i in three]
    out += [(i, j, 0) for j in three for i in three]
    out += [(0, 0, k) for k in three] + [(0, j, 0) for j in three] + [(i, 0, 0) for i in three]
    return out


OFFS = offsets()


def split3(rows):
    high = rows.astype(bf16)
    rest = rows - high.astype(f32)
    mid = rest.astype(bf16)
    low = (rest - mid.astype(f32)).astype(bf16)
    return high, mid, low


def col_stack(rows):
    h, m, l = split3(rows)
    one = jnp.ones((16, HALF), bf16)
    return jnp.concatenate([h, h, m, m, h, l, one, jnp.zeros_like(one)], 0)


def row_stack(rows, sq):
    h, m, l = split3(rows)
    row = lax.broadcasted_iota(jnp.int32, (16, HALF), 0)
    last = jnp.zeros((16, HALF), f32)
    for n, part in enumerate(split3(sq)):
        last = jnp.where(row == n, part.astype(f32), last)
    return jnp.concatenate([h, m, h, m, l, h, last.astype(bf16), jnp.zeros((16, HALF), bf16)], 0)


def vec_stack(rows):
    high = rows.astype(bf16).astype(f32)
    return jnp.concatenate([high, rows - high], 0).astype(bf16)


def tile_of(t):
    t = jnp.maximum(t, 1e-30)
    w = -LIFT - t * lax.rsqrt(t)
    return (w * w + SHIFT) * jnp.exp2(w)


def mv(x, k):
    return jnp.dot(x, k, preferred_element_type=f32)


def fold(acc):
    return acc[0:VEC] + acc[VEC : 2 * VEC]


def kernel(
    pts, inv, scale, noise, sol, res, dirn,
    outs,
    gath, rgath, igath, fgath, isnd, fsnd,
    qtmp, qmat, khi, klo, acc_d, acc_r, acc_i, dots,
    ex_p, ex_s, ex_r, sc_s, sc_r,
    s_line, r_line, s_run, r_run, s_one, r_one,
    s_i, r_i, s_f, r_f, s_x, r_x,
):
    g, m = lax.axis_index("grp"), lax.axis_index("mem")
    x, y, z, core = g // 8, (g // 2) % 4, (m // 2) * 2 + g % 2, m % 2
    partner = (g, (m // 2) * 2 + 1 - core)

    def peer(e1, e2, e3, other=0):
        px = (x + e1 + core * (e3 - e1)) % 4
        py = (y + e2) % 4
        pz = (z + e3 + core * (e1 - e3)) % 4
        return ((px * 4 + py) * 2 + pz % 2, (pz // 2) * 2 + (1 - core if other else core))

    barrier = pltpu.get_barrier_semaphore()

    def greet(device):
        pl.semaphore_signal(barrier, inc=1, device_id=device, device_id_type=MESH)

    greet(partner)
    for e in (1, 3, 2):
        greet(peer(e, 0, 0))
        greet(peer(0, e, 0))
        greet(peer(0, 0, e))

    gain = math.sqrt(5.0) * LOG2E
    own, r_own = gath.at[0, 0, 0], rgath.at[0, 0, 0]
    r_own[...] = res[...]
    for half, (at, at_sq) in enumerate(((16, 27), (29, 28))):
        lanes = slice(half * HALF, (half + 1) * HALF)
        own[8 * half : 8 * half + 8, :] = dirn[:, lanes]
        sq = jnp.zeros((1, HALF), f32)
        for f in range(FEAT):
            scaled = pts[f : f + 1, lanes] * (inv[f] * gain)
            own[at + f : at + f + 1, :] = scaled
            sq = sq + scaled * scaled
        own[at_sq : at_sq + 1, :] = sq

    def put(src, dst, s, r, device):
        cp = pltpu.make_async_remote_copy(
            src_ref=src, dst_ref=dst, send_sem=s, recv_sem=r, device_id=device, device_id_type=MESH
        )
        cp.start()
        return cp

    def await_(ref, sem):
        pltpu.make_async_copy(ref, ref, sem).wait()

    def exchange(n, src, dst):
        return put(src, dst, s_x.at[n], r_x.at[n], partner)

    bufs = gath, rgath

    def run(w, e3, e2):
        return bufs[w].at[e3, e2, pl.ds(1, 3)]

    def one(w, e3, e2):
        return bufs[w].at[e3, e2, 0]

    def put_run(w, src, e3, e2, device):
        n = 4 * e3 + e2
        put(run(w, *src), run(w, e3, e2), s_run.at[w, n], r_run.at[w, n], device)

    def put_one(w, src, e3, e2, device):
        n = 4 * e3 + e2
        put(one(w, *src), one(w, e3, e2), s_one.at[w, n], r_one.at[w, n], device)

    def await_run(w, e3, e2):
        await_(run(w, 0, 0), r_run.at[w, 4 * e3 + e2])

    def await_one(w, e3, e2):
        await_(one(w, 0, 0), r_one.at[w, 4 * e3 + e2])

    def leave(w):
        for e in (1, 3, 2):
            put(one(w, 0, 0), bufs[w].at[0, 0, e], s_line.at[w, e], r_line.at[w, e], peer(e, 0, 0))
            put_one(w, (0, 0), 0, e, peer(0, e, 0))
            put_one(w, (0, 0), e, 0, peer(0, 0, e))

    def pass_lines(w):
        for e in (1, 3, 2):
            await_(one(w, 0, 0), r_line.at[w, e])
        for e in (1, 3, 2):
            put_run(w, (0, 0), 0, e, peer(0, e, 0))
            put_run(w, (0, 0), e, 0, peer(0, 0, e))
        for e in (1, 3, 2):
            await_one(w, 0, e)
            for f in (1, 3, 2):
                put_one(w, (0, e), f, e, peer(0, 0, f))
        for e in (1, 3, 2):
            await_one(w, e, 0)

    def pass_planes(w):
        for e in (1, 3, 2):
            await_run(w, 0, e)
            for f in (1, 3, 2):
                put_run(w, (0, e), f, e, peer(0, 0, f))

    pl.semaphore_wait(barrier, 10)
    cp_p = exchange(0, own.at[pl.ds(16, 24)], ex_p)
    leave(0)
    leave(1)

    def rows_side(blk, top, start):
        for half, (at, at_sq) in enumerate(((16, 27), (29, 28))):
            p = -2.0 * blk[at - top : at - top + FEAT, :]
            sq = blk[at_sq - top : at_sq - top + 1, :]
            for cols, (put_at, one_at) in enumerate(((0, 11), (5, 4))):
                qtmp[...] = jnp.zeros_like(qtmp)
                qtmp[put_at : put_at + FEAT, :] = p
                qtmp[one_at : one_at + 1, :] = jnp.ones((1, HALF), f32)
                lanes = slice(start + half * HALF, start + (half + 1) * HALF)
                qmat[cols, :, lanes] = row_stack(qtmp[...], sq)

    for acc in (acc_d, acc_r, acc_i):
        acc[...] = jnp.zeros_like(acc)
    rows_side(own, 0, 0)
    cp_p.wait()
    rows_side(ex_p, 16, COLS)

    def build(places):
        for e3, e2, e1 in places:
            k = e3 * 16 + e2 * 4 + e1
            blk = gath.at[e3, e2, e1]
            cols = col_stack(blk[16:32, :]), col_stack(blk[24:40, :])
            vec = vec_stack(blk[0:8, :]), vec_stack(blk[8:16, :])
            for i0 in range(0, 2 * COLS, 256):
                part = acc_d[:, i0 : i0 + 256]
                for half in (0, 1):
                    j0 = half * HALF
                    t = lax.dot_general(
                        cols[half], qmat[half, :, i0 : i0 + 256],
                        (((0,), (0,)), ((), ())), preferred_element_type=f32,
                    )
                    tile = tile_of(t)
                    hi = tile.astype(bf16)
                    lo = (tile - hi.astype(f32)).astype(bf16)
                    khi[k, j0 : j0 + HALF, i0 : i0 + 256] = hi
                    klo[k, j0 : j0 + HALF, i0 : i0 + 256] = lo
                    part = part + mv(vec[half], hi) + mv(vec[half], lo)
                acc_d[:, i0 : i0 + 256] = part

    def times(acc, places, rows_of):
        for i0 in range(0, 2 * COLS, 256):
            part = acc[:, i0 : i0 + 256]
            for e3, e2, e1 in places:
                k = e3 * 16 + e2 * 4 + e1
                v = vec_stack(rows_of(e3, e2, e1))
                part = part + mv(v, khi[k, :, i0 : i0 + 256]) + mv(v, klo[k, :, i0 : i0 + 256])
            acc[:, i0 : i0 + 256] = part

    def pick(grp, *cases):
        out = cases[-1]
        for n in range(len(cases) - 2, -1, -1):
            out = jnp.where(grp == n, cases[n], out)
        return out

    def third(grp):
        return pick(grp, 0, 0, 0, 0, 1, 3, 2)

    def places_of(grp):
        e = third(grp)
        return [
            (
                pick(grp, p if q == 3 else 0, 0, q, q, e),
                pick(grp, p if q == 2 else 0, q, 0, p, q),
                pick(grp, p if q == 1 else 0, p, p, 0, p),
            )
            for q in range(1, 4)
            for p in range(1, 4)
        ]

    build([(0, 0, 0)])

    pass_lines(0)

    @pl.loop(0, GROUPS)
    def _(grp):
        @pl.when(grp == 1)
        def _():
            pass_planes(0)
            pass_lines(1)

        @pl.when(grp == 2)
        def _():
            for e in (1, 3, 2):
                await_run(0, e, 0)

        @pl.when(grp == 3)
        def _():
            for e in (1, 3, 2):
                for f in (1, 3, 2):
                    await_one(0, e, f)
            pass_planes(1)

        @pl.when(grp >= 4)
        def _():
            for f in (1, 3, 2):
                await_run(0, third(grp), f)

        build(places_of(grp))

    total = fold(acc_d[...])
    ex_s[0] = total[:, COLS:]
    cp_a = exchange(1, ex_s.at[0], ex_r.at[0])
    times(acc_r, [(0, 0, 0)], lambda e3, e2, e1: rgath[e3, e2, e1])
    cp_a.wait()
    kd = (SCALE * scale[0]) * (total[:, :COLS] + ex_r[0])
    image = kd + noise[0] * dirn[...]
    isnd[...] = image
    igath[0, 0, 0] = image
    for n, (e1, e2, e3) in enumerate(OFFS):
        put(isnd, igath.at[e3, e2, e1], s_i.at[0], r_i.at[e3 * 16 + e2 * 4 + e1], peer(e1, e2, e3))

    for e in (1, 3, 2):
        await_run(1, e, 0)
        for f in (1, 3, 2):
            await_one(1, e, f)
            await_run(1, e, f)

    @pl.loop(0, GROUPS)
    def _(grp):
        times(acc_r, places_of(grp), lambda e3, e2, e1: rgath[e3, e2, e1])

    def squares(step):
        def one_step(k, acc):
            v = step(k // 16, (k // 4) % 4, k % 4)
            return acc + v

        return lax.fori_loop(0, CHIPS, one_step, jnp.zeros((VEC, COLS), f32), unroll=8)

    def r_of(e3, e2, e1):
        return rgath[e3, e2, e1]

    rr = squares(lambda *e: r_of(*e) * r_of(*e))
    times(acc_i, [(0, 0, 0)], lambda e3, e2, e1: igath[e3, e2, e1])
    dots[...] = dirn[...] * image

    def meet(places):
        di = dots[...]
        for e3, e2, e1 in places:
            await_(isnd, r_i.at[e3 * 16 + e2 * 4 + e1])
        for e3, e2, e1 in places:
            blk = gath.at[e3, e2, e1]
            d = jnp.concatenate([blk[0:8, :], blk[8:16, :]], 1)
            di = di + d * igath[e3, e2, e1]
        dots[...] = di

    @pl.loop(0, GROUPS - 1)
    def _(back):
        places = places_of(GROUPS - 1 - back)
        meet(places)
        times(acc_i, places, lambda e3, e2, e1: igath[e3, e2, e1])

    lane = lax.broadcasted_iota(jnp.int32, (VEC, 128), 1)
    sub = lax.broadcasted_iota(jnp.int32, (VEC, 128), 0)

    def pack(*cols):
        out = jnp.zeros((VEC, 128), f32)
        for n, c in enumerate(cols):
            out = jnp.where(lane == n * VEC + sub, c, out)
        return jnp.sum(out, axis=0, keepdims=True)

    def take(a, n):
        return jnp.sum(jnp.where(lane == n * VEC + sub, a, 0.0), axis=1, keepdims=True)

    def total_of(a):
        return jnp.sum(a, axis=1, keepdims=True)

    lines = [(k, 0, 0) for k in (2, 3, 1)] + [(0, j, 0) for j in (2, 3, 1)] + [(0, 0, i) for i in (2, 3, 1)]
    meet(lines)
    mine = pack(total_of(rr), total_of(dots[...]))
    sc_s[0] = mine
    cp_b = exchange(2, sc_s.at[0], sc_r.at[0])
    times(acc_i, lines, lambda e3, e2, e1: igath[e3, e2, e1])
    cp_b.wait()
    both = mine + sc_r[0]
    norm0 = take(both, 0)
    alpha0 = norm0 / take(both, 1)

    def r1_sq(e3, e2, e1):
        r1 = r_of(e3, e2, e1) - alpha0 * igath[e3, e2, e1]
        return r1 * r1

    mine = pack(total_of(squares(r1_sq)))
    sc_s[1] = mine
    cp_c = exchange(3, sc_s.at[1], sc_r.at[1])
    part = fold(acc_r[...]) - alpha0 * fold(acc_i[...])
    ex_s[1] = part[:, COLS:]
    cp_d = exchange(4, ex_s.at[1], ex_r.at[1])
    cp_c.wait()
    norm1 = take(mine + sc_r[1], 0)
    beta = norm1 / norm0
    r1 = res[...] - alpha0 * image
    d1 = r1 + beta * dirn[...]
    cp_d.wait()
    im1 = (SCALE * scale[0]) * (part[:, :COLS] + ex_r[1]) + beta * kd + noise[0] * d1
    mine = pack(total_of(d1 * im1), total_of(r1 * im1), total_of(im1 * im1))
    fsnd[...] = mine
    fgath[0] = mine
    for other in (0, 1):
        for e1, e2, e3 in OFFS + [(0, 0, 0)] * other:
            k = other * CHIPS + e3 * 16 + e2 * 4 + e1
            put(fsnd, fgath.at[k], s_f.at[0], r_f.at[k], peer(e1, e2, e3, other))

    sol1 = sol[...] + alpha0 * dirn[...]
    for w in (0, 1):
        for e in range(1, 4):
            await_(one(w, 0, 0), s_line.at[w, e])
        for e in range(1, 16):
            await_(one(w, 0, 0), s_one.at[w, e])
            await_(run(w, 0, 0), s_run.at[w, e])
    flat = igath.at[pl.ds(1, 3)], igath.at[0, pl.ds(1, 3)], igath.at[0, 0, pl.ds(1, 3)]
    for ref in flat:
        await_(ref, s_i.at[0])

    for k in range(1, 2 * CHIPS):
        await_(fsnd, r_f.at[k])
    both = jnp.sum(fgath[...], axis=0)
    alpha1 = norm1 / take(both, 0)
    norm2 = norm1 + alpha1 * (alpha1 * take(both, 2) - 2.0 * take(both, 1))
    r2 = r1 - alpha1 * im1
    outs[0:8, :] = sol1 + alpha1 * d1
    outs[8:16, :] = r2
    outs[16:24, :] = r2 + (norm2 / norm1) * d1
    await_(fgath.at[pl.ds(1, 2 * CHIPS - 1)], s_f.at[0])


def per_device(points, inv_length, out_scale, noise, solution, residual, direction):
    vm = pl.BlockSpec(memory_space=pltpu.VMEM)
    sm = pl.BlockSpec(memory_space=pltpu.SMEM)
    V, D = pltpu.VMEM, pltpu.SemaphoreType.DMA
    out = pl.pallas_call(
        kernel,
        out_shape=jax.ShapeDtypeStruct((3 * VEC, COLS), f32),
        in_specs=[vm, sm, sm, sm, vm, vm, vm],
        out_specs=vm,
        scratch_shapes=[
            V((4, 4, 4, 40, HALF), f32), V((4, 4, 4, VEC, COLS), f32), V((4, 4, 4, VEC, COLS), f32),
            V((2 * CHIPS, 1, 128), f32), V((VEC, COLS), f32), V((1, 128), f32),
            V((16, HALF), f32), V((2, 128, 2 * COLS), bf16),
            V((CHIPS, COLS, 2 * COLS), bf16), V((CHIPS, COLS, 2 * COLS), bf16),
            V((16, 2 * COLS), f32), V((16, 2 * COLS), f32), V((16, 2 * COLS), f32),
            V((VEC, COLS), f32),
            V((24, HALF), f32), V((2, VEC, COLS), f32), V((2, VEC, COLS), f32),
            V((2, 1, 128), f32), V((2, 1, 128), f32),
            D((2, 4)), D((2, 4)), D((2, 16)), D((2, 16)), D((2, 16)), D((2, 16)),
            D((1,)), D((CHIPS,)), D((1,)), D((2 * CHIPS,)), D((5,)), D((5,)),
        ],
        compiler_params=pltpu.CompilerParams(
            collective_id=0, has_side_effects=True, vmem_limit_bytes=56 * 2**20
        ),
        name="cg",
    )(points, inv_length, out_scale, noise, solution, residual, direction)
    return out[0:8], out[8:16], out[16:24]


def solution(mesh):
    cols = P(None, ("grp", "mem"))
    return jax.shard_map(
        per_device,
        mesh=mesh,
        in_specs=(cols, P(), P(), P(), cols, cols, cols),
        out_specs=(cols, cols, cols),
        check_vma=False,
    )
```

time: 65.4 us -> 61.9 us (0.946)
  Pallas kernels: 60.6 us -> 58.4 us
  local copies, waits for them, and re-layouts: 2.6 us -> 1.34 us
    unnamed x7 -> x0, local copies, waits for them, and re-layouts: 2.6 us -> none
    pallas_call x1, Pallas kernels: 60.6 us -> 58.4 us  [per_device(): pl.pallas_call(kernel, out_shape=jax.ShapeDtypeStruct((3 * VEC, COLS), f3...]
    slice x0 -> x1, local copies, waits for them, and re-layouts: none -> 1.34 us  [per_device(): return (out[0:8], out[8:16], out[16:24])]
where the time goes in v3:
time: 61.9 us; the launch traced here: 61.7 us
  Pallas kernels  58.4 us (94%)
  between operations  1.93 us (3%)
  local copies, waits for them, and re-layouts  1.34 us (2%)
    pallas_call x1, Pallas kernels, per_device(): pl.pallas_call(kernel, out_shape=jax.ShapeDtypeStruct((3 * VEC, COLS), f3...  58.4 us
    slice x1, local copies, waits for them, and re-layouts, per_device(): return (out[0:8], out[8:16], out[16:24])  1.34 us

profile of v3, /device:TPU:1, one launch (start us, length us, event | category | flops | bytes accessed | tf_op | source)
XLA Modules:
  0.0 61.7 jit_solution(2032376041926771737)
XLA Ops:
  1.9 58.4 %cg.1 = f32[24,256]{1,0:T(8,128)} custom-call(f32[11,256]{1,0:T(8,128)} %pts.1, f32[11]{0:T(128)} %inv.1, f32[1]{0:T(128)S(6)} %copy.10.scale, f32[1]{0:T(128)S(6)} %copy.11.noise, f32[8,256]{1,0:T(8,128)} %sol.1, f32[8,256]{1,0:T(8,128)} %res.1, f32[8,256]{1,0:T(8,128)} %dirn.1), custom_call_target="tpu_custom_call" | custom-call | tf_op jit(solution)/shard_map/cg/pallas_call | solution.py:418
  60.4 1.3 %fusion = (f32[8,256]{1,0:T(8,128)}, f32[8,256]{1,0:T(8,128)}, f32[8,256]{1,0:T(8,128)}) fusion(f32[24,256]{1,0:T(8,128)} %cg.1), kind=kLoop, calls=%fused_computation | loop fusion | bytes 49152 | tf_op jit(solution)/shard_map/slice | solution.py:440

commit v4 on v3

--- a/solution.py
+++ b/solution.py
@@ -79,13 +79,14 @@
 
 
 def kernel(
-    pts, inv, scale, noise, sol, res, dirn,
+    pts_in, inv, scale, noise, sol_in, res_in, dirn_in,
     outs,
     gath, rgath, igath, fgath, isnd, fsnd,
     qtmp, qmat, khi, klo, acc_d, acc_r, acc_i, dots,
     ex_p, ex_s, ex_r, sc_s, sc_r,
     s_line, r_line, s_run, r_run, s_one, r_one,
-    s_i, r_i, s_f, r_f, s_x, r_x,
+    s_i, r_i, s_f, r_f, s_x, r_x, s_alt, r_alt,
+    pts, sol, res, dirn, s_in,
 ):
     g, m = lax.axis_index("grp"), lax.axis_index("mem")
     x, y, z, core = g // 8, (g // 2) % 4, (m // 2) * 2 + g % 2, m % 2
@@ -97,6 +98,10 @@
         pz = (z + e3 + core * (e1 - e3)) % 4
         return ((px * 4 + py) * 2 + pz % 2, (pz // 2) * 2 + (1 - core if other else core))
 
+    loads = (pts_in, pts), (dirn_in, dirn), (res_in, res), (sol_in, sol)
+    loads = [pltpu.make_async_copy(a, b, s_in.at[n]) for n, (a, b) in enumerate(loads)]
+    for cp in loads:
+        cp.start()
     barrier = pltpu.get_barrier_semaphore()
 
     def greet(device):
@@ -110,6 +115,8 @@
 
     gain = math.sqrt(5.0) * LOG2E
     own, r_own = gath.at[0, 0, 0], rgath.at[0, 0, 0]
+    for cp in loads:
+        cp.wait()
     r_own[...] = res[...]
     for half, (at, at_sq) in enumerate(((16, 27), (29, 28))):
         lanes = slice(half * HALF, (half + 1) * HALF)
@@ -142,16 +149,30 @@
     def one(w, e3, e2):
         return bufs[w].at[e3, e2, 0]
 
-    def put_run(w, src, e3, e2, device):
+    def run_from(w, e3, e2):
+        return run(w, e3, e2) if 0 in (e3, e2) else bufs[w].at[e3, e2, pl.ds(2, 2)]
+
+    def put_run(w, e3, e2, device):
+        src = run(w, 0, 0) if 0 in (e3, e2) else run_from(w, 0, e2).at[pl.ds(1, 2)]
         n = 4 * e3 + e2
-        put(run(w, *src), run(w, e3, e2), s_run.at[w, n], r_run.at[w, n], device)
+        put(src, run_from(w, e3, e2), s_run.at[w, n], r_run.at[w, n], device)
+
+    def put_alt(w, e3, e2, device):
+        n = 4 * e3 + e2
+        put(bufs[w].at[e3, 0, 1], bufs[w].at[e3, e2, 1], s_alt.at[w, n], r_alt.at[w, n], device)
 
     def put_one(w, src, e3, e2, device):
         n = 4 * e3 + e2
         put(one(w, *src), one(w, e3, e2), s_one.at[w, n], r_one.at[w, n], device)
 
     def await_run(w, e3, e2):
-        await_(run(w, 0, 0), r_run.at[w, 4 * e3 + e2])
+        await_(run_from(w, e3, e2), r_run.at[w, 4 * e3 + e2])
+
+    def await_far(w, e3):
+        for e2 in (1, 3, 2):
+            n = 4 * e3 + e2
+            await_(bufs[w].at[0, 0, pl.ds(2, 2)], r_run.at[w, n])
+            await_(one(w, 0, 0), r_alt.at[w, n])
 
     def await_one(w, e3, e2):
         await_(one(w, 0, 0), r_one.at[w, 4 * e3 + e2])
@@ -165,12 +186,13 @@
     def pass_lines(w):
         for e in (1, 3, 2):
             await_(one(w, 0, 0), r_line.at[w, e])
-        for e in (1, 3, 2):
-            put_run(w, (0, 0), 0, e, peer(0, e, 0))
-            put_run(w, (0, 0), e, 0, peer(0, 0, e))
+        for e in (2, 1, 3):
+            put_run(w, 0, e, peer(0, e, 0))
+        for e in (2, 1, 3):
+            put_run(w, e, 0, peer(0, 0, e))
         for e in (1, 3, 2):
             await_one(w, 0, e)
-            for f in (1, 3, 2):
+            for f in (2, 1, 3):
                 put_one(w, (0, e), f, e, peer(0, 0, f))
         for e in (1, 3, 2):
             await_one(w, e, 0)
@@ -179,12 +201,11 @@
         for e in (1, 3, 2):
             await_run(w, 0, e)
             for f in (1, 3, 2):
-                put_run(w, (0, e), f, e, peer(0, 0, f))
-
-    pl.semaphore_wait(barrier, 10)
-    cp_p = exchange(0, own.at[pl.ds(16, 24)], ex_p)
-    leave(0)
-    leave(1)
+                put_run(w, f, e, peer(0, 0, f))
+        for e in (1, 3, 2):
+            await_run(w, e, 0)
+            for f in (2, 1, 3):
+                put_alt(w, e, f, peer(0, f, 0))
 
     def rows_side(blk, top, start):
         for half, (at, at_sq) in enumerate(((16, 27), (29, 28))):
@@ -200,9 +221,11 @@
     for acc in (acc_d, acc_r, acc_i):
         acc[...] = jnp.zeros_like(acc)
     rows_side(own, 0, 0)
+    pl.semaphore_wait(barrier, 10)
+    cp_p = exchange(0, own.at[pl.ds(16, 24)], ex_p)
+    leave(0)
     cp_p.wait()
     rows_side(ex_p, 16, COLS)
-
     def build(places):
         for e3, e2, e1 in places:
             k = e3 * 16 + e2 * 4 + e1
@@ -256,8 +279,8 @@
         ]
 
     build([(0, 0, 0)])
-
     pass_lines(0)
+    leave(1)
 
     @pl.loop(0, GROUPS)
     def _(grp):
@@ -266,11 +289,6 @@
             pass_planes(0)
             pass_lines(1)
 
-        @pl.when(grp == 2)
-        def _():
-            for e in (1, 3, 2):
-                await_run(0, e, 0)
-
         @pl.when(grp == 3)
         def _():
             for e in (1, 3, 2):
@@ -280,8 +298,7 @@
 
         @pl.when(grp >= 4)
         def _():
-            for f in (1, 3, 2):
-                await_run(0, third(grp), f)
+            await_far(0, third(grp))
 
         build(places_of(grp))
 
@@ -298,10 +315,9 @@
         put(isnd, igath.at[e3, e2, e1], s_i.at[0], r_i.at[e3 * 16 + e2 * 4 + e1], peer(e1, e2, e3))
 
     for e in (1, 3, 2):
-        await_run(1, e, 0)
+        await_far(1, e)
         for f in (1, 3, 2):
             await_one(1, e, f)
-            await_run(1, e, f)
 
     @pl.loop(0, GROUPS)
     def _(grp):
@@ -394,7 +410,9 @@
             await_(one(w, 0, 0), s_line.at[w, e])
         for e in range(1, 16):
             await_(one(w, 0, 0), s_one.at[w, e])
-            await_(run(w, 0, 0), s_run.at[w, e])
+            await_(run_from(w, e // 4, e % 4), s_run.at[w, e])
+            if e // 4 and e % 4:
+                await_(one(w, 0, 0), s_alt.at[w, e])
     flat = igath.at[pl.ds(1, 3)], igath.at[0, pl.ds(1, 3)], igath.at[0, 0, pl.ds(1, 3)]
     for ref in flat:
         await_(ref, s_i.at[0])
@@ -413,12 +431,13 @@
 
 def per_device(points, inv_length, out_scale, noise, solution, residual, direction):
     vm = pl.BlockSpec(memory_space=pltpu.VMEM)
+    hbm = pl.BlockSpec(memory_space=pl.ANY)
     sm = pl.BlockSpec(memory_space=pltpu.SMEM)
     V, D = pltpu.VMEM, pltpu.SemaphoreType.DMA
     out = pl.pallas_call(
         kernel,
         out_shape=jax.ShapeDtypeStruct((3 * VEC, COLS), f32),
-        in_specs=[vm, sm, sm, sm, vm, vm, vm],
+        in_specs=[hbm, sm, sm, sm, hbm, hbm, hbm],
         out_specs=vm,
         scratch_shapes=[
             V((4, 4, 4, 40, HALF), f32), V((4, 4, 4, VEC, COLS), f32), V((4, 4, 4, VEC, COLS), f32),
@@ -430,7 +449,8 @@
             V((24, HALF), f32), V((2, VEC, COLS), f32), V((2, VEC, COLS), f32),
             V((2, 1, 128), f32), V((2, 1, 128), f32),
             D((2, 4)), D((2, 4)), D((2, 16)), D((2, 16)), D((2, 16)), D((2, 16)),
-            D((1,)), D((CHIPS,)), D((1,)), D((2 * CHIPS,)), D((5,)), D((5,)),
+            D((1,)), D((CHIPS,)), D((1,)), D((2 * CHIPS,)), D((5,)), D((5,)), D((2, 16)), D((2, 16)),
+            V((FEAT, COLS), f32), V((VEC, COLS), f32), V((VEC, COLS), f32), V((VEC, COLS), f32), D((4,)),
         ],
         compiler_params=pltpu.CompilerParams(
             collective_id=0, has_side_effects=True, vmem_limit_bytes=56 * 2**20

time: 61.9 us -> 63.6 us (1.027)
  Pallas kernels: 58.4 us -> 60.1 us
    pallas_call x1, Pallas kernels: 58.4 us -> 60.1 us  [per_device(): pl.pallas_call(kernel, out_shape=jax.ShapeDtypeStruct((3 * VEC, COLS), f3...]
where the time goes in v4:
time: 63.6 us; the launch traced here: 63.3 us
  Pallas kernels  60.1 us (94%)
  between operations  1.93 us (3%)
  local copies, waits for them, and re-layouts  1.34 us (2%)
    pallas_call x1, Pallas kernels, per_device(): pl.pallas_call(kernel, out_shape=jax.ShapeDtypeStruct((3 * VEC, COLS), f3...  60.1 us
    slice x1, local copies, waits for them, and re-layouts, per_device(): return (out[0:8], out[8:16], out[16:24])  1.34 us

profile of v4, /device:TPU:1, one launch (start us, length us, event | category | flops | bytes accessed | tf_op | source)
XLA Modules:
  0.0 63.3 jit_solution(17054156878922664661)
XLA Ops:
  1.9 60.1 %cg.1 = f32[24,256]{1,0:T(8,128)} custom-call(f32[11,256]{1,0:T(8,128)} %pts_in.1, f32[11]{0:T(128)} %inv.1, f32[1]{0:T(128)S(6)} %copy.10.scale, f32[1]{0:T(128)S(6)} %copy.11.noise, f32[8,256]{1,0:T(8,128)} %sol_in.1, f32[8,256]{1,0:T(8,128)} %res_in.1, f32[8,256]{1,0:T(8,128)} %dirn_in.1), custom_call_target="tpu_custom_call" | custom-call | tf_op jit(solution)/shard_map/cg/pallas_call | solution.py:437
  62.0 1.3 %fusion = (f32[8,256]{1,0:T(8,128)}, f32[8,256]{1,0:T(8,128)}, f32[8,256]{1,0:T(8,128)}) fusion(f32[24,256]{1,0:T(8,128)} %cg.1), kind=kLoop, calls=%fused_computation | loop fusion | bytes 49152 | tf_op jit(solution)/shard_map/slice | solution.py:460

commit v5 on v3

--- a/solution.py
+++ b/solution.py
@@ -34,6 +34,7 @@
 
 
 OFFS = offsets()
+PLANE = [(1, 1), (3, 3), (1, 3), (3, 1), (2, 1), (1, 2), (2, 3), (3, 2), (2, 2)]
 
 
 def split3(rows):
@@ -79,13 +80,13 @@
 
 
 def kernel(
-    pts, inv, scale, noise, sol, res, dirn,
+    pts_in, inv, scale, noise, sol_in, res_in, dirn_in,
     outs,
     gath, rgath, igath, fgath, isnd, fsnd,
     qtmp, qmat, khi, klo, acc_d, acc_r, acc_i, dots,
     ex_p, ex_s, ex_r, sc_s, sc_r,
-    s_line, r_line, s_run, r_run, s_one, r_one,
-    s_i, r_i, s_f, r_f, s_x, r_x,
+    s_blk, r_blk, s_i, r_i, s_f, r_f, s_x, r_x,
+    pts, sol, res, dirn, s_in,
 ):
     g, m = lax.axis_index("grp"), lax.axis_index("mem")
     x, y, z, core = g // 8, (g // 2) % 4, (m // 2) * 2 + g % 2, m % 2
@@ -97,6 +98,10 @@
         pz = (z + e3 + core * (e1 - e3)) % 4
         return ((px * 4 + py) * 2 + pz % 2, (pz // 2) * 2 + (1 - core if other else core))
 
+    loads = (pts_in, pts), (dirn_in, dirn), (res_in, res), (sol_in, sol)
+    loads = [pltpu.make_async_copy(a, b, s_in.at[n]) for n, (a, b) in enumerate(loads)]
+    for cp in loads:
+        cp.start()
     barrier = pltpu.get_barrier_semaphore()
 
     def greet(device):
@@ -107,10 +112,13 @@
         greet(peer(e, 0, 0))
         greet(peer(0, e, 0))
         greet(peer(0, 0, e))
+    for e1, e2 in PLANE:
+        greet(peer(e1, e2, 0))
 
     gain = math.sqrt(5.0) * LOG2E
     own, r_own = gath.at[0, 0, 0], rgath.at[0, 0, 0]
-    r_own[...] = res[...]
+    for cp in loads[:2]:
+        cp.wait()
     for half, (at, at_sq) in enumerate(((16, 27), (29, 28))):
         lanes = slice(half * HALF, (half + 1) * HALF)
         own[8 * half : 8 * half + 8, :] = dirn[:, lanes]
@@ -136,72 +144,67 @@
 
     bufs = gath, rgath
 
-    def run(w, e3, e2):
-        return bufs[w].at[e3, e2, pl.ds(1, 3)]
-
-    def one(w, e3, e2):
-        return bufs[w].at[e3, e2, 0]
-
-    def put_run(w, src, e3, e2, device):
-        n = 4 * e3 + e2
-        put(run(w, *src), run(w, e3, e2), s_run.at[w, n], r_run.at[w, n], device)
-
-    def put_one(w, src, e3, e2, device):
-        n = 4 * e3 + e2
-        put(one(w, *src), one(w, e3, e2), s_one.at[w, n], r_one.at[w, n], device)
-
-    def await_run(w, e3, e2):
-        await_(run(w, 0, 0), r_run.at[w, 4 * e3 + e2])
-
-    def await_one(w, e3, e2):
-        await_(one(w, 0, 0), r_one.at[w, 4 * e3 + e2])
+    def send(w, src, dst, n, device):
+        put(bufs[w].at[src], bufs[w].at[dst], s_blk.at[w], r_blk.at[w, n], device)
+
+    def nine(w, n):
+        await_(bufs[w].at[pl.ds(0, 3), pl.ds(0, 3), 0], r_blk.at[w, n])
 
     def leave(w):
         for e in (1, 3, 2):
-            put(one(w, 0, 0), bufs[w].at[0, 0, e], s_line.at[w, e], r_line.at[w, e], peer(e, 0, 0))
-            put_one(w, (0, 0), 0, e, peer(0, e, 0))
-            put_one(w, (0, 0), e, 0, peer(0, 0, e))
+            send(w, (0, 0, 0), (0, 0, e), 0, peer(e, 0, 0))
+            send(w, (0, 0, 0), (0, e, 0), 0, peer(0, e, 0))
+        for e in (1, 3, 2):
+            send(w, (0, 0, 0), (e, 0, 0), 1, peer(0, 0, e))
+        for e1, e2 in PLANE:
+            send(w, (0, 0, 0), (0, e2, e1), 2, peer(e1, e2, 0))
 
     def pass_lines(w):
-        for e in (1, 3, 2):
-            await_(one(w, 0, 0), r_line.at[w, e])
-        for e in (1, 3, 2):
-            put_run(w, (0, 0), 0, e, peer(0, e, 0))
-            put_run(w, (0, 0), e, 0, peer(0, 0, e))
-        for e in (1, 3, 2):
-            await_one(w, 0, e)
-            for f in (1, 3, 2):
-                put_one(w, (0, e), f, e, peer(0, 0, f))
-        for e in (1, 3, 2):
-            await_one(w, e, 0)
-
-    def pass_planes(w):
-        for e in (1, 3, 2):
-            await_run(w, 0, e)
-            for f in (1, 3, 2):
-                put_run(w, (0, e), f, e, peer(0, 0, f))
-
-    pl.semaphore_wait(barrier, 10)
+        await_(bufs[w].at[pl.ds(0, 2), pl.ds(0, 3), 0], r_blk.at[w, 0])
+        for f in (1, 3, 2):
+            send(w, (0, 0, pl.ds(1, 3)), (f, 0, pl.ds(1, 3)), 3, peer(0, 0, f))
+        for f in (1, 3, 2):
+            for e in (1, 3, 2):
+                send(w, (0, e, 0), (f, e, 0), 4, peer(0, 0, f))
+        await_(bufs[w].at[pl.ds(0, 3), 0, 0], r_blk.at[w, 1])
+
+    def pass_plane(w):
+        nine(w, 2)
+        for f in (1, 3, 2):
+            for e in (1, 3, 2):
+                send(w, (0, e, pl.ds(2, 2)), (f, e, pl.ds(2, 2)), 4 + f, peer(0, 0, f))
+
+    def pass_second(w):
+        nine(w, 3)
+        for f in (1, 3, 2):
+            for e in (1, 3, 2):
+                send(w, (f, 0, 1), (f, e, 1), 4 + f, peer(0, e, 0))
+
+    def rows_side(blk, top, start, n):
+        pairs = [(half, cols) for half in (0, 1) for cols in (0, 1)]
+        for half, cols in pairs:
+            at = (16, 29)[half] - top
+            put_at, one_at = ((0, 11), (5, 4))[cols]
+            tmp = qtmp.at[n + 2 * half + cols]
+            tmp[put_at : put_at + FEAT, :] = -2.0 * blk[at : at + FEAT, :]
+            tmp[one_at : one_at + 1, :] = jnp.ones((1, HALF), f32)
+        for half, cols in pairs:
+            at_sq = (27, 28)[half] - top
+            lanes = slice(start + half * HALF, start + (half + 1) * HALF)
+            rows = qtmp[n + 2 * half + cols]
+            qmat[cols, :, lanes] = row_stack(rows, blk[at_sq : at_sq + 1, :])
+
+    pl.semaphore_wait(barrier, 19)
     cp_p = exchange(0, own.at[pl.ds(16, 24)], ex_p)
     leave(0)
-    leave(1)
-
-    def rows_side(blk, top, start):
-        for half, (at, at_sq) in enumerate(((16, 27), (29, 28))):
-            p = -2.0 * blk[at - top : at - top + FEAT, :]
-            sq = blk[at_sq - top : at_sq - top + 1, :]
-            for cols, (put_at, one_at) in enumerate(((0, 11), (5, 4))):
-                qtmp[...] = jnp.zeros_like(qtmp)
-                qtmp[put_at : put_at + FEAT, :] = p
-                qtmp[one_at : one_at + 1, :] = jnp.ones((1, HALF), f32)
-                lanes = slice(start + half * HALF, start + (half + 1) * HALF)
-                qmat[cols, :, lanes] = row_stack(qtmp[...], sq)
-
-    for acc in (acc_d, acc_r, acc_i):
+    for acc in (acc_d, acc_r, acc_i, qtmp):
         acc[...] = jnp.zeros_like(acc)
-    rows_side(own, 0, 0)
+    rows_side(own, 0, 0, 0)
+    for cp in loads[2:]:
+        cp.wait()
+    r_own[...] = res[...]
     cp_p.wait()
-    rows_side(ex_p, 16, COLS)
+    rows_side(ex_p, 16, COLS, 4)
 
     def build(places):
         for e3, e2, e1 in places:
@@ -256,32 +259,38 @@
         ]
 
     build([(0, 0, 0)])
-
     pass_lines(0)
 
     @pl.loop(0, GROUPS)
     def _(grp):
         @pl.when(grp == 1)
         def _():
-            pass_planes(0)
+            pass_plane(0)
+
+        @pl.when(grp == 2)
+        def _():
+            pass_second(0)
+            leave(1)
+
+        @pl.when(grp == 3)
+        def _():
+            nine(0, 4)
+
+        @pl.when(grp >= 4)
+        def _():
+            nine(0, 4 + third(grp))
+
+        @pl.when(grp == 4)
+        def _():
             pass_lines(1)
 
-        @pl.when(grp == 2)
-        def _():
-            for e in (1, 3, 2):
-                await_run(0, e, 0)
-
-        @pl.when(grp == 3)
-        def _():
-            for e in (1, 3, 2):
-                for f in (1, 3, 2):
-                    await_one(0, e, f)
-            pass_planes(1)
-
-        @pl.when(grp >= 4)
-        def _():
-            for f in (1, 3, 2):
-                await_run(0, third(grp), f)
+        @pl.when(grp == 5)
+        def _():
+            pass_plane(1)
+
+        @pl.when(grp == 6)
+        def _():
+            pass_second(1)
 
         build(places_of(grp))
 
@@ -295,13 +304,10 @@
     isnd[...] = image
     igath[0, 0, 0] = image
     for n, (e1, e2, e3) in enumerate(OFFS):
-        put(isnd, igath.at[e3, e2, e1], s_i.at[0], r_i.at[e3 * 16 + e2 * 4 + e1], peer(e1, e2, e3))
-
-    for e in (1, 3, 2):
-        await_run(1, e, 0)
-        for f in (1, 3, 2):
-            await_one(1, e, f)
-            await_run(1, e, f)
+        put(isnd, igath.at[e3, e2, e1], s_i.at[0], r_i.at[n // 9], peer(e1, e2, e3))
+
+    for n in range(4, 8):
+        nine(1, n)
 
     @pl.loop(0, GROUPS)
     def _(grp):
@@ -321,10 +327,9 @@
     times(acc_i, [(0, 0, 0)], lambda e3, e2, e1: igath[e3, e2, e1])
     dots[...] = dirn[...] * image
 
-    def meet(places):
+    def meet(places, n):
         di = dots[...]
-        for e3, e2, e1 in places:
-            await_(isnd, r_i.at[e3 * 16 + e2 * 4 + e1])
+        await_(igath.at[pl.ds(0, 3), pl.ds(0, 3), 0], r_i.at[n])
         for e3, e2, e1 in places:
             blk = gath.at[e3, e2, e1]
             d = jnp.concatenate([blk[0:8, :], blk[8:16, :]], 1)
@@ -334,7 +339,7 @@
     @pl.loop(0, GROUPS - 1)
     def _(back):
         places = places_of(GROUPS - 1 - back)
-        meet(places)
+        meet(places, back)
         times(acc_i, places, lambda e3, e2, e1: igath[e3, e2, e1])
 
     lane = lax.broadcasted_iota(jnp.int32, (VEC, 128), 1)
@@ -353,7 +358,7 @@
         return jnp.sum(a, axis=1, keepdims=True)
 
     lines = [(k, 0, 0) for k in (2, 3, 1)] + [(0, j, 0) for j in (2, 3, 1)] + [(0, 0, i) for i in (2, 3, 1)]
-    meet(lines)
+    meet(lines, GROUPS - 1)
     mine = pack(total_of(rr), total_of(dots[...]))
     sc_s[0] = mine
     cp_b = exchange(2, sc_s.at[0], sc_r.at[0])
@@ -386,21 +391,19 @@
     for other in (0, 1):
         for e1, e2, e3 in OFFS + [(0, 0, 0)] * other:
             k = other * CHIPS + e3 * 16 + e2 * 4 + e1
-            put(fsnd, fgath.at[k], s_f.at[0], r_f.at[k], peer(e1, e2, e3, other))
+            put(fsnd, fgath.at[k], s_f.at[0], r_f.at[0], peer(e1, e2, e3, other))
 
     sol1 = sol[...] + alpha0 * dirn[...]
+    def others(ref):
+        return ref.at[pl.ds(1, 3)], ref.at[0, pl.ds(1, 3)], ref.at[0, 0, pl.ds(1, 3)]
+
     for w in (0, 1):
-        for e in range(1, 4):
-            await_(one(w, 0, 0), s_line.at[w, e])
-        for e in range(1, 16):
-            await_(one(w, 0, 0), s_one.at[w, e])
-            await_(run(w, 0, 0), s_run.at[w, e])
-    flat = igath.at[pl.ds(1, 3)], igath.at[0, pl.ds(1, 3)], igath.at[0, 0, pl.ds(1, 3)]
-    for ref in flat:
+        for ref in others(bufs[w]):
+            await_(ref, s_blk.at[w])
+    for ref in others(igath):
         await_(ref, s_i.at[0])
 
-    for k in range(1, 2 * CHIPS):
-        await_(fsnd, r_f.at[k])
+    await_(fgath.at[pl.ds(1, 2 * CHIPS - 1)], r_f.at[0])
     both = jnp.sum(fgath[...], axis=0)
     alpha1 = norm1 / take(both, 0)
     norm2 = norm1 + alpha1 * (alpha1 * take(both, 2) - 2.0 * take(both, 1))
@@ -413,24 +416,25 @@
 
 def per_device(points, inv_length, out_scale, noise, solution, residual, direction):
     vm = pl.BlockSpec(memory_space=pltpu.VMEM)
+    hbm = pl.BlockSpec(memory_space=pl.ANY)
     sm = pl.BlockSpec(memory_space=pltpu.SMEM)
     V, D = pltpu.VMEM, pltpu.SemaphoreType.DMA
     out = pl.pallas_call(
         kernel,
         out_shape=jax.ShapeDtypeStruct((3 * VEC, COLS), f32),
-        in_specs=[vm, sm, sm, sm, vm, vm, vm],
+        in_specs=[hbm, sm, sm, sm, hbm, hbm, hbm],
         out_specs=vm,
         scratch_shapes=[
             V((4, 4, 4, 40, HALF), f32), V((4, 4, 4, VEC, COLS), f32), V((4, 4, 4, VEC, COLS), f32),
             V((2 * CHIPS, 1, 128), f32), V((VEC, COLS), f32), V((1, 128), f32),
-            V((16, HALF), f32), V((2, 128, 2 * COLS), bf16),
+            V((8, 16, HALF), f32), V((2, 128, 2 * COLS), bf16),
             V((CHIPS, COLS, 2 * COLS), bf16), V((CHIPS, COLS, 2 * COLS), bf16),
             V((16, 2 * COLS), f32), V((16, 2 * COLS), f32), V((16, 2 * COLS), f32),
             V((VEC, COLS), f32),
             V((24, HALF), f32), V((2, VEC, COLS), f32), V((2, VEC, COLS), f32),
             V((2, 1, 128), f32), V((2, 1, 128), f32),
-            D((2, 4)), D((2, 4)), D((2, 16)), D((2, 16)), D((2, 16)), D((2, 16)),
-            D((1,)), D((CHIPS,)), D((1,)), D((2 * CHIPS,)), D((5,)), D((5,)),
+            D((2,)), D((2, 8)), D((1,)), D((GROUPS,)), D((1,)), D((1,)), D((5,)), D((5,)),
+            V((FEAT, COLS), f32), V((VEC, COLS), f32), V((VEC, COLS), f32), V((VEC, COLS), f32), D((4,)),
         ],
         compiler_params=pltpu.CompilerParams(
             collective_id=0, has_side_effects=True, vmem_limit_bytes=56 * 2**20

time: 61.9 us -> 58.5 us (0.945)
  Pallas kernels: 58.4 us -> 54.9 us
    pallas_call x1, Pallas kernels: 58.4 us -> 54.9 us  [per_device(): pl.pallas_call(kernel, out_shape=jax.ShapeDtypeStruct((3 * VEC, COLS), f3...]
where the time goes in v5:
time: 58.5 us; the launch traced here: 58.2 us
  Pallas kernels  54.9 us (94%)
  between operations  1.93 us (3%)
  local copies, waits for them, and re-layouts  1.34 us (2%)
    pallas_call x1, Pallas kernels, per_device(): pl.pallas_call(kernel, out_shape=jax.ShapeDtypeStruct((3 * VEC, COLS), f3...  54.9 us
    slice x1, local copies, waits for them, and re-layouts, per_device(): return (out[0:8], out[8:16], out[16:24])  1.34 us

profile of v5, /device:TPU:1, one launch (start us, length us, event | category | flops | bytes accessed | tf_op | source)
XLA Modules:
  0.0 58.2 jit_solution(2727535354172586618)
XLA Ops:
  1.9 54.9 %cg.1 = f32[24,256]{1,0:T(8,128)} custom-call(f32[11,256]{1,0:T(8,128)} %pts_in.1, f32[11]{0:T(128)} %inv.1, f32[1]{0:T(128)S(6)} %copy.10.scale, f32[1]{0:T(128)S(6)} %copy.11.noise, f32[8,256]{1,0:T(8,128)} %sol_in.1, f32[8,256]{1,0:T(8,128)} %res_in.1, f32[8,256]{1,0:T(8,128)} %dirn_in.1), custom_call_target="tpu_custom_call" | custom-call | tf_op jit(solution)/shard_map/cg/pallas_call | solution.py:422
  56.9 1.3 %fusion = (f32[8,256]{1,0:T(8,128)}, f32[8,256]{1,0:T(8,128)}, f32[8,256]{1,0:T(8,128)}) fusion(f32[24,256]{1,0:T(8,128)} %cg.1), kind=kLoop, calls=%fused_computation | loop fusion | bytes 49152 | tf_op jit(solution)/shard_map/slice | solution.py:444

commit v6 on v5

--- a/solution.py
+++ b/solution.py
@@ -83,7 +83,7 @@
     pts_in, inv, scale, noise, sol_in, res_in, dirn_in,
     outs,
     gath, rgath, igath, fgath, isnd, fsnd,
-    qtmp, qmat, khi, klo, acc_d, acc_r, acc_i, dots,
+    qtmp, qmat, khi, klo, acc_d, acc_r, acc_i,
     ex_p, ex_s, ex_r, sc_s, sc_r,
     s_blk, r_blk, s_i, r_i, s_f, r_f, s_x, r_x,
     pts, sol, res, dirn, s_in,
@@ -206,13 +206,13 @@
     cp_p.wait()
     rows_side(ex_p, 16, COLS, 4)
 
-    def build(places):
+    def build(places, starts=(0, 256)):
         for e3, e2, e1 in places:
             k = e3 * 16 + e2 * 4 + e1
             blk = gath.at[e3, e2, e1]
             cols = col_stack(blk[16:32, :]), col_stack(blk[24:40, :])
             vec = vec_stack(blk[0:8, :]), vec_stack(blk[8:16, :])
-            for i0 in range(0, 2 * COLS, 256):
+            for i0 in starts:
                 part = acc_d[:, i0 : i0 + 256]
                 for half in (0, 1):
                     j0 = half * HALF
@@ -228,8 +228,8 @@
                     part = part + mv(vec[half], hi) + mv(vec[half], lo)
                 acc_d[:, i0 : i0 + 256] = part
 
-    def times(acc, places, rows_of):
-        for i0 in range(0, 2 * COLS, 256):
+    def times(acc, places, rows_of, starts=(0, 256)):
+        for i0 in starts:
             part = acc[:, i0 : i0 + 256]
             for e3, e2, e1 in places:
                 k = e3 * 16 + e2 * 4 + e1
@@ -261,7 +261,7 @@
     build([(0, 0, 0)])
     pass_lines(0)
 
-    @pl.loop(0, GROUPS)
+    @pl.loop(0, GROUPS - 1)
     def _(grp):
         @pl.when(grp == 1)
         def _():
@@ -288,60 +288,25 @@
         def _():
             pass_plane(1)
 
-        @pl.when(grp == 6)
-        def _():
-            pass_second(1)
-
         build(places_of(grp))
 
-    total = fold(acc_d[...])
-    ex_s[0] = total[:, COLS:]
+    last = [(2, j, i) for j in range(1, 4) for i in range(1, 4)]
+    nine(0, 6)
+    pass_second(1)
+    build(last, (256,))
+    ex_s[0] = fold(acc_d[:, COLS:])
     cp_a = exchange(1, ex_s.at[0], ex_r.at[0])
-    times(acc_r, [(0, 0, 0)], lambda e3, e2, e1: rgath[e3, e2, e1])
+    build(last, (0,))
+    total = fold(acc_d[:, :COLS])
     cp_a.wait()
-    kd = (SCALE * scale[0]) * (total[:, :COLS] + ex_r[0])
+
+    kd = (SCALE * scale[0]) * (total + ex_r[0])
     image = kd + noise[0] * dirn[...]
     isnd[...] = image
     igath[0, 0, 0] = image
     for n, (e1, e2, e3) in enumerate(OFFS):
         put(isnd, igath.at[e3, e2, e1], s_i.at[0], r_i.at[n // 9], peer(e1, e2, e3))
 
-    for n in range(4, 8):
-        nine(1, n)
-
-    @pl.loop(0, GROUPS)
-    def _(grp):
-        times(acc_r, places_of(grp), lambda e3, e2, e1: rgath[e3, e2, e1])
-
-    def squares(step):
-        def one_step(k, acc):
-            v = step(k // 16, (k // 4) % 4, k % 4)
-            return acc + v
-
-        return lax.fori_loop(0, CHIPS, one_step, jnp.zeros((VEC, COLS), f32), unroll=8)
-
-    def r_of(e3, e2, e1):
-        return rgath[e3, e2, e1]
-
-    rr = squares(lambda *e: r_of(*e) * r_of(*e))
-    times(acc_i, [(0, 0, 0)], lambda e3, e2, e1: igath[e3, e2, e1])
-    dots[...] = dirn[...] * image
-
-    def meet(places, n):
-        di = dots[...]
-        await_(igath.at[pl.ds(0, 3), pl.ds(0, 3), 0], r_i.at[n])
-        for e3, e2, e1 in places:
-            blk = gath.at[e3, e2, e1]
-            d = jnp.concatenate([blk[0:8, :], blk[8:16, :]], 1)
-            di = di + d * igath[e3, e2, e1]
-        dots[...] = di
-
-    @pl.loop(0, GROUPS - 1)
-    def _(back):
-        places = places_of(GROUPS - 1 - back)
-        meet(places, back)
-        times(acc_i, places, lambda e3, e2, e1: igath[e3, e2, e1])
-
     lane = lax.broadcasted_iota(jnp.int32, (VEC, 128), 1)
     sub = lax.broadcasted_iota(jnp.int32, (VEC, 128), 0)
 
@@ -357,41 +322,95 @@
     def total_of(a):
         return jnp.sum(a, axis=1, keepdims=True)
 
-    lines = [(k, 0, 0) for k in (2, 3, 1)] + [(0, j, 0) for j in (2, 3, 1)] + [(0, 0, i) for i in (2, 3, 1)]
-    meet(lines, GROUPS - 1)
-    mine = pack(total_of(rr), total_of(dots[...]))
+    def tell(row, src, dst, s, r):
+        src[...] = row
+        dst[0] = row
+        for other in (0, 1):
+            for e1, e2, e3 in OFFS + [(0, 0, 0)] * other:
+                k = other * CHIPS + e3 * 16 + e2 * 4 + e1
+                put(src, dst.at[k], s.at[0], r.at[0], peer(e1, e2, e3, other))
+
+    def told(dst, r):
+        await_(dst.at[pl.ds(1, 2 * CHIPS - 1)], r.at[0])
+        return jnp.sum(dst[...], axis=0)
+
+
+    times(acc_r, [(0, 0, 0)], lambda e3, e2, e1: rgath[e3, e2, e1])
+    for n in range(4, 8):
+        nine(1, n)
+
+    @pl.loop(0, GROUPS)
+    def _(grp):
+        times(acc_r, places_of(grp), lambda e3, e2, e1: rgath[e3, e2, e1])
+
+    def image_of(e3, e2, e1):
+        return igath[e3, e2, e1]
+
+    def met(n):
+        await_(igath.at[pl.ds(0, 3), pl.ds(0, 3), 0], r_i.at[n])
+
+    times(acc_i, [(0, 0, 0)], image_of)
+
+    def sums(acc, places):
+        rr, di = acc
+        for e3, e2, e1 in places:
+            blk, r = gath.at[e3, e2, e1], rgath[e3, e2, e1]
+            d = jnp.concatenate([blk[0:8, :], blk[8:16, :]], 1)
+            rr = rr + r * r
+            di = di + d * igath[e3, e2, e1]
+        return rr, di
+
+    def r1_sq(acc, places):
+        for e3, e2, e1 in places:
+            v = rgath[e3, e2, e1] - alpha0 * igath[e3, e2, e1]
+            acc = acc + v * v
+        return acc
+
+    EARLY = 4
+
+    @pl.loop(0, EARLY)
+    def _(back):
+        met(back)
+        times(acc_i, places_of(GROUPS - 1 - back), image_of)
+
+    late = [
+        [(j, 0, i) for j in range(1, 4) for i in range(1, 4)],
+        [(0, j, i) for j in range(1, 4) for i in range(1, 4)],
+        [(k, 0, 0) for k in (2, 3, 1)] + [(0, j, 0) for j in (2, 3, 1)] + [(0, 0, i) for i in (2, 3, 1)],
+    ]
+    zero = jnp.zeros((VEC, COLS), f32)
+    full = [(j, i) for j in range(4) for i in range(4)]
+    deep = [(j, i) for j in range(1, 4) for i in range(4)]
+    acc = lax.fori_loop(1, 4, lambda k, acc: sums(acc, [(k, j, i) for j, i in deep]), (zero, zero))
+    acc = sums(acc, [(0, 0, 0)])
+    for n, places in enumerate(late):
+        met(EARLY + n)
+        acc = sums(acc, places)
+    mine = pack(total_of(acc[0]), total_of(acc[1]))
     sc_s[0] = mine
     cp_b = exchange(2, sc_s.at[0], sc_r.at[0])
-    times(acc_i, lines, lambda e3, e2, e1: igath[e3, e2, e1])
+    times(acc_i, late[0] + late[1], image_of)
     cp_b.wait()
     both = mine + sc_r[0]
     norm0 = take(both, 0)
     alpha0 = norm0 / take(both, 1)
-
-    def r1_sq(e3, e2, e1):
-        r1 = r_of(e3, e2, e1) - alpha0 * igath[e3, e2, e1]
-        return r1 * r1
-
-    mine = pack(total_of(squares(r1_sq)))
+    acc = lax.fori_loop(0, 4, lambda k, acc: r1_sq(acc, [(k, j, i) for j, i in full]), zero)
+    mine = pack(total_of(acc))
     sc_s[1] = mine
     cp_c = exchange(3, sc_s.at[1], sc_r.at[1])
-    part = fold(acc_r[...]) - alpha0 * fold(acc_i[...])
-    ex_s[1] = part[:, COLS:]
+    times(acc_i, late[2], image_of, (256,))
+    ex_s[1] = fold(acc_r[:, COLS:]) - alpha0 * fold(acc_i[:, COLS:])
     cp_d = exchange(4, ex_s.at[1], ex_r.at[1])
+    times(acc_i, late[2], image_of, (0,))
+    part = fold(acc_r[:, :COLS]) - alpha0 * fold(acc_i[:, :COLS])
+    r1 = res[...] - alpha0 * image
     cp_c.wait()
     norm1 = take(mine + sc_r[1], 0)
     beta = norm1 / norm0
-    r1 = res[...] - alpha0 * image
     d1 = r1 + beta * dirn[...]
     cp_d.wait()
-    im1 = (SCALE * scale[0]) * (part[:, :COLS] + ex_r[1]) + beta * kd + noise[0] * d1
-    mine = pack(total_of(d1 * im1), total_of(r1 * im1), total_of(im1 * im1))
-    fsnd[...] = mine
-    fgath[0] = mine
-    for other in (0, 1):
-        for e1, e2, e3 in OFFS + [(0, 0, 0)] * other:
-            k = other * CHIPS + e3 * 16 + e2 * 4 + e1
-            put(fsnd, fgath.at[k], s_f.at[0], r_f.at[0], peer(e1, e2, e3, other))
+    im1 = (SCALE * scale[0]) * (part + ex_r[1]) + beta * kd + noise[0] * d1
+    tell(pack(total_of(d1 * im1), total_of(r1 * im1), total_of(im1 * im1)), fsnd, fgath, s_f, r_f)
 
     sol1 = sol[...] + alpha0 * dirn[...]
     def others(ref):
@@ -403,8 +422,8 @@
     for ref in others(igath):
         await_(ref, s_i.at[0])
 
-    await_(fgath.at[pl.ds(1, 2 * CHIPS - 1)], r_f.at[0])
-    both = jnp.sum(fgath[...], axis=0)
+
+    both = told(fgath, r_f)
     alpha1 = norm1 / take(both, 0)
     norm2 = norm1 + alpha1 * (alpha1 * take(both, 2) - 2.0 * take(both, 1))
     r2 = r1 - alpha1 * im1
@@ -430,7 +449,6 @@
             V((8, 16, HALF), f32), V((2, 128, 2 * COLS), bf16),
             V((CHIPS, COLS, 2 * COLS), bf16), V((CHIPS, COLS, 2 * COLS), bf16),
             V((16, 2 * COLS), f32), V((16, 2 * COLS), f32), V((16, 2 * COLS), f32),
-            V((VEC, COLS), f32),
             V((24, HALF), f32), V((2, VEC, COLS), f32), V((2, VEC, COLS), f32),
             V((2, 1, 128), f32), V((2, 1, 128), f32),
             D((2,)), D((2, 8)), D((1,)), D((GROUPS,)), D((1,)), D((1,)), D((5,)), D((5,)),

time: 58.5 us -> 56.6 us (0.968)
  Pallas kernels: 54.9 us -> 53.1 us
    pallas_call x1, Pallas kernels: 54.9 us -> 53.1 us  [per_device(): pl.pallas_call(kernel, out_shape=jax.ShapeDtypeStruct((3 * VEC, COLS), f3...]
where the time goes in v6:
time: 56.6 us; the launch traced here: 56.4 us
  Pallas kernels  53.1 us (94%)
  between operations  1.93 us (3%)
  local copies, waits for them, and re-layouts  1.34 us (2%)
    pallas_call x1, Pallas kernels, per_device(): pl.pallas_call(kernel, out_shape=jax.ShapeDtypeStruct((3 * VEC, COLS), f3...  53.1 us
    slice x1, local copies, waits for them, and re-layouts, per_device(): return (out[0:8], out[8:16], out[16:24])  1.34 us

profile of v6, /device:TPU:1, one launch (start us, length us, event | category | flops | bytes accessed | tf_op | source)
XLA Modules:
  0.0 56.4 jit_solution(16579704248777343643)
XLA Ops:
  1.9 53.1 %cg.1 = f32[24,256]{1,0:T(8,128)} custom-call(f32[11,256]{1,0:T(8,128)} %pts_in.1, f32[11]{0:T(128)} %inv.1, f32[1]{0:T(128)S(6)} %copy.10.scale, f32[1]{0:T(128)S(6)} %copy.11.noise, f32[8,256]{1,0:T(8,128)} %sol_in.1, f32[8,256]{1,0:T(8,128)} %res_in.1, f32[8,256]{1,0:T(8,128)} %dirn_in.1), custom_call_target="tpu_custom_call" | custom-call | tf_op jit(solution)/shard_map/cg/pallas_call | solution.py:441
  55.0 1.3 %fusion = (f32[8,256]{1,0:T(8,128)}, f32[8,256]{1,0:T(8,128)}, f32[8,256]{1,0:T(8,128)}) fusion(f32[24,256]{1,0:T(8,128)} %cg.1), kind=kLoop, calls=%fused_computation | loop fusion | bytes 49152 | tf_op jit(solution)/shard_map/slice | solution.py:462

commit v7 on v6

--- a/solution.py
+++ b/solution.py
@@ -34,6 +34,12 @@
 
 
 OFFS = offsets()
+
+
+def hops(off):
+    return sum((0, 1, 2, 1)[d] for d in off)
+
+
 PLANE = [(1, 1), (3, 3), (1, 3), (3, 1), (2, 1), (1, 2), (2, 3), (3, 2), (2, 2)]
 
 
@@ -172,13 +178,7 @@
         nine(w, 2)
         for f in (1, 3, 2):
             for e in (1, 3, 2):
-                send(w, (0, e, pl.ds(2, 2)), (f, e, pl.ds(2, 2)), 4 + f, peer(0, 0, f))
-
-    def pass_second(w):
-        nine(w, 3)
-        for f in (1, 3, 2):
-            for e in (1, 3, 2):
-                send(w, (f, 0, 1), (f, e, 1), 4 + f, peer(0, e, 0))
+                send(w, (0, e, pl.ds(1, 3)), (f, e, pl.ds(1, 3)), 4 + f, peer(0, 0, f))
 
     def rows_side(blk, top, start, n):
         pairs = [(half, cols) for half in (0, 1) for cols in (0, 1)]
@@ -269,30 +269,26 @@
 
         @pl.when(grp == 2)
         def _():
-            pass_second(0)
+            nine(0, 3)
+
+        @pl.when(grp == 3)
+        def _():
+            nine(0, 4)
             leave(1)
 
-        @pl.when(grp == 3)
-        def _():
-            nine(0, 4)
-
         @pl.when(grp >= 4)
         def _():
             nine(0, 4 + third(grp))
 
-        @pl.when(grp == 4)
+        @pl.when(grp == 5)
         def _():
             pass_lines(1)
-
-        @pl.when(grp == 5)
-        def _():
-            pass_plane(1)
 
         build(places_of(grp))
 
     last = [(2, j, i) for j in range(1, 4) for i in range(1, 4)]
     nine(0, 6)
-    pass_second(1)
+    pass_plane(1)
     build(last, (256,))
     ex_s[0] = fold(acc_d[:, COLS:])
     cp_a = exchange(1, ex_s.at[0], ex_r.at[0])
@@ -325,10 +321,10 @@
     def tell(row, src, dst, s, r):
         src[...] = row
         dst[0] = row
-        for other in (0, 1):
-            for e1, e2, e3 in OFFS + [(0, 0, 0)] * other:
-                k = other * CHIPS + e3 * 16 + e2 * 4 + e1
-                put(src, dst.at[k], s.at[0], r.at[0], peer(e1, e2, e3, other))
+        every = [(e, other) for other in (0, 1) for e in OFFS + [(0, 0, 0)] * other]
+        for (e1, e2, e3), other in sorted(every, key=lambda e: -hops(e[0])):
+            k = other * CHIPS + e3 * 16 + e2 * 4 + e1
+            put(src, dst.at[k], s.at[0], r.at[0], peer(e1, e2, e3, other))
 
     def told(dst, r):
         await_(dst.at[pl.ds(1, 2 * CHIPS - 1)], r.at[0])
@@ -336,11 +332,18 @@
 
 
     times(acc_r, [(0, 0, 0)], lambda e3, e2, e1: rgath[e3, e2, e1])
-    for n in range(4, 8):
-        nine(1, n)
+    nine(1, 3)
 
     @pl.loop(0, GROUPS)
     def _(grp):
+        @pl.when(grp == 3)
+        def _():
+            nine(1, 4)
+
+        @pl.when(grp >= 4)
+        def _():
+            nine(1, 4 + third(grp))
+
         times(acc_r, places_of(grp), lambda e3, e2, e1: rgath[e3, e2, e1])
 
     def image_of(e3, e2, e1):

time: 56.6 us -> 55.5 us (0.981)
  Pallas kernels: 53.1 us -> 52 us
    pallas_call x1, Pallas kernels: 53.1 us -> 52 us  [per_device(): pl.pallas_call(kernel, out_shape=jax.ShapeDtypeStruct((3 * VEC, COLS), f3...]
where the time goes in v7:
time: 55.5 us; the launch traced here: 55.3 us
  Pallas kernels  52 us (94%)
  between operations  1.93 us (3%)
  local copies, waits for them, and re-layouts  1.34 us (2%)
    pallas_call x1, Pallas kernels, per_device(): pl.pallas_call(kernel, out_shape=jax.ShapeDtypeStruct((3 * VEC, COLS), f3...  52 us
    slice x1, local copies, waits for them, and re-layouts, per_device(): return (out[0:8], out[8:16], out[16:24])  1.34 us

profile of v7, /device:TPU:1, one launch (start us, length us, event | category | flops | bytes accessed | tf_op | source)
XLA Modules:
  0.0 55.3 jit_solution(5386350822821657044)
XLA Ops:
  1.9 52.0 %cg.1 = f32[24,256]{1,0:T(8,128)} custom-call(f32[11,256]{1,0:T(8,128)} %pts_in.1, f32[11]{0:T(128)} %inv.1, f32[1]{0:T(128)S(6)} %copy.10.scale, f32[1]{0:T(128)S(6)} %copy.11.noise, f32[8,256]{1,0:T(8,128)} %sol_in.1, f32[8,256]{1,0:T(8,128)} %res_in.1, f32[8,256]{1,0:T(8,128)} %dirn_in.1), custom_call_target="tpu_custom_call" | custom-call | tf_op jit(solution)/shard_map/cg/pallas_call | solution.py:444
  53.9 1.3 %fusion = (f32[8,256]{1,0:T(8,128)}, f32[8,256]{1,0:T(8,128)}, f32[8,256]{1,0:T(8,128)}) fusion(f32[24,256]{1,0:T(8,128)} %cg.1), kind=kLoop, calls=%fused_computation | loop fusion | bytes 49152 | tf_op jit(solution)/shard_map/slice | solution.py:465

commit v8 on v7

--- a/solution.py
+++ b/solution.py
@@ -98,11 +98,17 @@
     x, y, z, core = g // 8, (g // 2) % 4, (m // 2) * 2 + g % 2, m % 2
     partner = (g, (m // 2) * 2 + 1 - core)
 
+    at_x = [((x + e) % 4) * 8 for e in range(4)]
+    at_y = [((y + e) % 4) * 2 for e in range(4)]
+    at_z = [(z + e) % 4 for e in range(4)]
+    odd_z = [v % 2 for v in at_z]
+    high_z = [(v // 2) * 2 for v in at_z]
+    both = [(i, j) for i in range(4) for j in range(4)]
+    outer = {(i, j): jnp.where(core == 0, at_x[i] + odd_z[j], at_x[j] + odd_z[i]) for i, j in both}
+    inner = {(i, j): jnp.where(core == 0, high_z[j], high_z[i]) for i, j in both}
+
     def peer(e1, e2, e3, other=0):
-        px = (x + e1 + core * (e3 - e1)) % 4
-        py = (y + e2) % 4
-        pz = (z + e3 + core * (e1 - e3)) % 4
-        return ((px * 4 + py) * 2 + pz % 2, (pz // 2) * 2 + (1 - core if other else core))
+        return (outer[e1, e3] + at_y[e2], inner[e1, e3] + (1 - core if other else core))
 
     loads = (pts_in, pts), (dirn_in, dirn), (res_in, res), (sol_in, sol)
     loads = [pltpu.make_async_copy(a, b, s_in.at[n]) for n, (a, b) in enumerate(loads)]

time: 55.5 us -> 55.4 us (level)
  no operation moved by 1% of the time
where the time goes in v8:
time: 55.4 us; the launch traced here: 55.2 us
  Pallas kernels  51.9 us (94%)
  between operations  1.93 us (3%)
  local copies, waits for them, and re-layouts  1.34 us (2%)
    pallas_call x1, Pallas kernels, per_device(): pl.pallas_call(kernel, out_shape=jax.ShapeDtypeStruct((3 * VEC, COLS), f3...  51.9 us
    slice x1, local copies, waits for them, and re-layouts, per_device(): return (out[0:8], out[8:16], out[16:24])  1.34 us

profile of v8, /device:TPU:1, one launch (start us, length us, event | category | flops | bytes accessed | tf_op | source)
XLA Modules:
  0.0 55.2 jit_solution(10525184425916796872)
XLA Ops:
  1.9 51.9 %cg.1 = f32[24,256]{1,0:T(8,128)} custom-call(f32[11,256]{1,0:T(8,128)} %pts_in.1, f32[11]{0:T(128)} %inv.1, f32[1]{0:T(128)S(6)} %copy.10.scale, f32[1]{0:T(128)S(6)} %copy.11.noise, f32[8,256]{1,0:T(8,128)} %sol_in.1, f32[8,256]{1,0:T(8,128)} %res_in.1, f32[8,256]{1,0:T(8,128)} %dirn_in.1), custom_call_target="tpu_custom_call" | custom-call | tf_op jit(solution)/shard_map/cg/pallas_call | solution.py:450
  53.8 1.3 %fusion = (f32[8,256]{1,0:T(8,128)}, f32[8,256]{1,0:T(8,128)}, f32[8,256]{1,0:T(8,128)}) fusion(f32[24,256]{1,0:T(8,128)} %cg.1), kind=kLoop, calls=%fused_computation | loop fusion | bytes 49152 | tf_op jit(solution)/shard_map/slice | solution.py:471
